TPU v7x, 32 devices: a whole 2x2x4 slice. The times are simulated.
32 devices in a mesh: section: 2 (over y), grp: 4 (over z), sta: 4 (over x, core).
Axes of the slice: x: 2, y: 2, z: 4, core: 2. Of those that a mesh axis runs over, the one named last changes fastest.
Arguments:
- records: bfloat16 [128, 4, 3, 16384], P(('section', 'grp', 'sta')), may hold values from -6 to 6
- fir_taps: float32 [64], replicated, may hold values from -0.75 to 0.75
- band_bins: int32 [4, 2], replicated, may hold values from 0 to 2048, as said below
- station_live: int32 [128], P(('section', 'grp', 'sta')), may hold values 0 or 1
- block_live: int32 [16], P(('section', 'grp')), may hold values 0 or 1
Outputs:
- correlations: float32 [2304, 16, 1024], P('sta', ('section', 'grp'))
Inputs may be any that keep to these rules, and one draw needn't show every extreme that they name: band_bins[b, 0] < band_bins[b, 1]; each band spans 64 to 256 bins.
All inputs are finite; a program needn't handle non-finite values. No bound on the sum of `station_live` or of `block_live` on one device may be relied on, other than what follows from the above.
Results may differ from a plain program's by a relative error of at most 0.0077.
Values may be sent and summed in bfloat16 or wider, within the bound.
No kernel may reach another device: no remote copies, remote signals or barrier semaphores. Data moves between devices by JAX's collectives and lax.ppermute only.
A program may use at most 64 MiB of HBM per device.

v0:
```python
import functools
import math

import jax
import jax.numpy as jnp
import numpy as np
from jax import lax
from jax.experimental import pallas as pl
from jax.experimental.pallas import tpu as pltpu
from jax.sharding import PartitionSpec as P

BINS = 2048
NT = 4096
DEC = 4
RAW = 16384
TAPS = 64
NBANDS = 4
SLOT = 256
OFFS = 2
LAGS = 1024
HALF = LAGS // 2
RADIX = 16
INNER = NT // RADIX
BIG = BINS // RADIX
FOLD = 256 // RADIX
FRAME = 128
SPAN = DEC * FRAME
LEAD = 256
WINDOW = SPAN + LEAD
PIECES = 4
BLOCKS_IN = NT // FRAME
KEPT = NBANDS * SLOT
EPS = 1e-06

f32 = jnp.float32
bf16 = jnp.bfloat16


def by_tile(table):
    padded = np.pad(table, ((0, 0), (0, -table.shape[1] % 128)))
    return np.ascontiguousarray(
        padded.reshape(table.shape[0], -1, 128).transpose(1, 0, 2)
    )


def joined(ref):
    return jnp.concatenate([ref[i] for i in range(ref.shape[0])], axis=1)


def split_const(table):
    high = table.astype(np.float32).astype(bf16)
    low = (table - high.astype(np.float64)).astype(np.float32).astype(bf16)
    return high, low


def compact_order():
    place = np.arange(SLOT)
    return RADIX * (place % FOLD) + place // FOLD


def spectra_constants():
    inner = np.arange(INNER)
    g = np.arange(BIG)
    angle = 2.0 * np.pi * ((inner[:, None] * g[None, :]) % INNER) / INNER
    cos, sin = np.cos(angle), np.sin(angle)
    table = np.concatenate(
        [np.concatenate([cos, -sin], axis=1), np.concatenate([sin, cos], axis=1)], axis=0
    )
    high, low = split_const(table)
    h = np.arange(RADIX)
    turn = 2.0 * np.pi * (h[:, None] * inner[None, :]) / NT
    twiddle = np.stack([np.cos(turn), -np.sin(turn)]).astype(np.float32)
    place = np.zeros((TAPS, WINDOW), np.float32)
    place[np.arange(TAPS), LEAD - np.arange(TAPS)] = 1.0
    fold = np.zeros((RADIX, BIG, SLOT), np.float32)
    for step in range(RADIX):
        fold[step, np.arange(BIG), FOLD * step + np.arange(BIG) % FOLD] = 1.0
    fold = by_tile(fold.reshape(BINS, SLOT).astype(bf16))
    return np.stack([by_tile(high), by_tile(low)]), twiddle, by_tile(place.astype(bf16)), fold


def lag_constants():
    q = compact_order()[:, None].astype(np.float64)
    n = np.arange(HALF)[None, :] + 0.5
    angle = 2.0 * np.pi * ((q * 2 * n) % (2 * NT)) / (2 * NT)
    base = np.stack([np.cos(angle), np.sin(angle)]) / math.sqrt(BINS)
    block = np.arange(16)[:, None].astype(np.float64)
    turn = 2.0 * np.pi * ((block * SLOT * 2 * n) % (2 * NT)) / (2 * NT)
    shift = np.stack([np.cos(turn), np.sin(turn)])
    return base.astype(np.float32), shift.astype(np.float32)


def real_dft8(d):
    r = math.sqrt(0.5)
    s = [d[b] + d[b + 4] for b in range(4)]
    t = [d[b] - d[b + 4] for b in range(4)]
    s02, s13 = s[0] + s[2], s[1] + s[3]
    t13m, t13p = r * (t[1] - t[3]), r * (t[1] + t[3])
    return [
        (s02 + s13, None),
        (t[0] + t13m, -(t[2] + t13p)),
        (s[0] - s[2], s[3] - s[1]),
        (t[0] - t13m, t[2] - t13p),
        (s02 - s13, None),
    ]


def real_dft16(d):
    even, odd = real_dft8(d[0::2]), real_dft8(d[1::2])
    y = [None] * 16
    y[0] = (even[0][0] + odd[0][0], None)
    y[8] = (even[0][0] - odd[0][0], None)
    y[4] = (even[4][0], -odd[4][0])
    for h in range(1, 4):
        c, s = math.cos(math.pi * h / 8), -math.sin(math.pi * h / 8)
        re, im = odd[h]
        tr, ti = re * c - im * s, re * s + im * c
        y[h] = (even[h][0] + tr, even[h][1] + ti)
        y[8 - h] = (even[h][0] - tr, ti - even[h][1])
    for h in range(9, 16):
        y[h] = (y[16 - h][0], -y[16 - h][1])
    return y


def spectra_kernel(
    x_hbm,
    taps_hbm,
    bands_hbm,
    live_hbm,
    table_hbm,
    twiddle_hbm,
    place_hbm,
    fold_hbm,
    order_hbm,
    sent_ref,
    x_ref,
    taps_ref,
    bands_ref,
    live_ref,
    table_ref,
    twiddle_ref,
    place_ref,
    fold_ref,
    order_ref,
    u_high,
    u_low,
    kept,
    sems,
):
    ch = x_ref.shape[0] * x_ref.shape[1]
    piece = RAW // PIECES
    pairs = [(taps_hbm, taps_ref), (place_hbm, place_ref)]
    for i in range(PIECES):
        lanes = slice(i * piece, (i + 1) * piece)
        pairs.append((x_hbm.at[:, :, lanes], x_ref.at[:, :, lanes]))
    pairs += [
        (twiddle_hbm, twiddle_ref),
        (table_hbm, table_ref),
        (bands_hbm, bands_ref),
        (live_hbm, live_ref),
        (fold_hbm, fold_ref),
        (order_hbm, order_ref),
    ]
    copies = [pltpu.make_async_copy(a, b, sems.at[i]) for i, (a, b) in enumerate(pairs)]
    for copy in copies:
        copy.start()
    copies[0].wait()
    taps = taps_ref[...]
    copies[1].wait()
    taps_high = taps.astype(bf16)
    taps_low = (taps - taps_high.astype(f32)).astype(bf16)

    def toeplitz(part):
        row = jnp.dot(part, joined(place_ref), preferred_element_type=f32)
        return pltpu.roll(
            jnp.broadcast_to(row, (FRAME, WINDOW)), 0, 1, stride=DEC, stride_axis=0
        ).astype(bf16)

    weights = jnp.concatenate([toeplitz(taps_high), toeplitz(taps_low)], axis=0)
    decimated = []
    tail = jnp.zeros((ch, LEAD), bf16)
    for i in range(PIECES):
        copies[2 + i].wait()
        x = x_ref[:, :, i * piece : (i + 1) * piece].reshape(ch, piece)
        x = jnp.concatenate([tail, x], axis=1)
        tail = x[:, piece:]
        windows = [x[:, at : at + WINDOW] for at in range(0, piece, SPAN)]
        both = lax.dot_general(
            jnp.concatenate(windows, axis=0),
            weights,
            (((1,), (1,)), ((), ())),
            preferred_element_type=f32,
        )
        decimated.append((both[:, :FRAME] + both[:, FRAME:]).astype(bf16).astype(f32))
    each = BLOCKS_IN // PIECES
    copies[2 + PIECES].wait()
    for at in range(0, ch, 16):
        d = []
        for b in range(RADIX):
            pair = []
            for frame in (2 * b, 2 * b + 1):
                row = frame % each * ch + at
                pair.append(decimated[frame // each][row : row + 16])
            d.append(jnp.concatenate(pair, axis=1))
        y = real_dft16(d)
        for h in range(RADIX):
            c = twiddle_ref[0, h : h + 1, :]
            sn = twiddle_ref[1, h : h + 1, :]
            yr, yi = y[h]
            if yi is None:
                ur, ui = yr * c, yr * sn
            else:
                ur, ui = yr * c - yi * sn, yr * sn + yi * c
            for k, u in enumerate((ur, ui)):
                where = slice(k * INNER, (k + 1) * INNER)
                top = u.astype(bf16)
                u_high[h * ch + at : h * ch + at + 16, where] = top
                u_low[h * ch + at : h * ch + at + 16, where] = (u - top.astype(f32)).astype(bf16)

    for copy in copies[3 + PIECES :]:
        copy.wait()
    table_high, table_low = joined(table_ref.at[0]), joined(table_ref.at[1])
    spectrum = (
        jnp.dot(u_high[...], table_high, preferred_element_type=f32)
        + jnp.dot(u_low[...], table_high, preferred_element_type=f32)
        + jnp.dot(u_high[...], table_low, preferred_element_type=f32)
    )

    row = lax.broadcasted_iota(jnp.int32, (ch, 1), 0)
    station = row // 12
    live = jnp.zeros((ch, 1), f32)
    station_live = live_ref[...].astype(f32)
    for s_at in range(live_ref.shape[1]):
        live = jnp.where(station == s_at, station_live[:, s_at : s_at + 1], live)
    bands = bands_ref[...]
    edges = [[bands[k : k + 1, b : b + 1] for b in range(NBANDS)] for k in range(2)]

    g = lax.broadcasted_iota(jnp.int32, (1, BIG), 1)
    inside = []
    for h in range(RADIX):
        f = RADIX * g + h
        inside.append(
            [
                ((f >= edges[0][b]) & (f < edges[1][b])).astype(f32)
                for b in range(NBANDS)
            ]
        )
    parts = []
    sums = [jnp.zeros((ch, BIG), f32) for _ in range(NBANDS)]
    for h in range(RADIX):
        re = spectrum[h * ch : (h + 1) * ch, :BIG]
        im = spectrum[h * ch : (h + 1) * ch, BIG:]
        parts.append((re, im))
        power = re * re + im * im
        for b in range(NBANDS):
            sums[b] = sums[b] + power * inside[h][b]
    gains = []
    for b in range(NBANDS):
        width = (edges[1][b] - edges[0][b]).astype(f32)
        energy = jnp.sum(sums[b], axis=1, keepdims=True) / width
        gains.append(lax.rsqrt(energy + EPS) * live)

    for h in range(0, RADIX, 2):
        own = []
        gain = [sum(inside[h + e][b] * gains[b] for b in range(NBANDS)) for e in range(2)]
        for b in range(NBANDS):
            pair = []
            for e in range(2):
                mask = inside[h + e][b]
                for earlier in range(b):
                    mask = mask * (1.0 - inside[h + e][earlier])
                pair.append(mask)
            own.append(jnp.concatenate(pair, axis=1).astype(bf16))
        for k in range(2):
            value = jnp.concatenate([parts[h + e][k] * gain[e] for e in range(2)], axis=1)
            value = value.astype(bf16)
            for b in range(NBANDS):
                at = (2 * b + k) * ch
                kept[at : at + ch, h * BIG : (h + 2) * BIG] = value * own[b]
    compact = jnp.dot(kept[...], joined(fold_ref), preferred_element_type=f32).astype(bf16)
    side = jnp.concatenate([compact[at : at + ch] for at in range(0, 2 * NBANDS * ch, ch)], axis=1)
    order = order_ref[...][:, :ch]
    ordered = jnp.dot(order, side, preferred_element_type=f32).astype(bf16)
    for b in range(NBANDS):
        for k in range(2):
            at = (2 * b + k) * SLOT
            sent_ref[k, :, b * SLOT : (b + 1) * SLOT] = ordered[:, at : at + SLOT]


def spectra(records, fir_taps, bands, station_live):
    ns, nw, nc, _ = records.shape
    x = jnp.transpose(records, (0, 2, 1, 3)).reshape(ns * nc, nw, RAW)
    groups = ns * nc
    padded = -(-groups // 4) * 4
    if padded != groups:
        x = jnp.pad(x, ((0, padded - groups), (0, 0), (0, 0)))
    ch = padded * nw
    hbm = pl.BlockSpec(memory_space=pltpu.HBM)
    operands = (x, fir_taps.reshape(1, TAPS), bands, station_live.reshape(1, ns))
    order = np.zeros((nw * groups, -(-ch // 128) * 128), np.float32)
    for w in range(nw):
        for i in range(groups):
            order[w * groups + i, i * nw + w] = 1.0
    operands += spectra_constants() + (order.astype(bf16),)
    return pl.pallas_call(
        spectra_kernel,
        out_shape=jax.ShapeDtypeStruct((2, nw * groups, KEPT), bf16),
        in_specs=[hbm] * len(operands),
        out_specs=pl.BlockSpec(memory_space=pltpu.VMEM),
        scratch_shapes=[pltpu.VMEM(o.shape, o.dtype) for o in operands]
        + [
            pltpu.VMEM((RADIX * ch, 2 * INNER), bf16),
            pltpu.VMEM((RADIX * ch, 2 * INNER), bf16),
            pltpu.VMEM((2 * NBANDS * ch, BINS), bf16),
            pltpu.SemaphoreType.DMA((len(operands) - 1 + PIECES,)),
        ],
        compiler_params=pltpu.CompilerParams(vmem_limit_bytes=62 * 2**20),
        cost_estimate=pl.CostEstimate(
            flops=3 * 10**9, bytes_accessed=5 * 2**20, transcendentals=0
        ),
        name="spectra",
    )(*operands)


def prepare_kernel(peers, bands_ref, sent_ref, turned_ref):
    _, nw, groups, group_rows, _ = turned_ref.shape
    repeats = group_rows // peers
    local_rows = groups * repeats
    place = lax.broadcasted_iota(jnp.int32, (1, SLOT), 1)
    residue = RADIX * (place % FOLD) + place // FOLD
    for b in range(NBANDS):
        start = bands_ref[0, b]
        f = start + ((residue - start) & (SLOT - 1))
        phase = f.astype(f32) * (math.pi / NT)
        c, sn = jnp.cos(phase), jnp.sin(phase)
        where = slice(b * SLOT, (b + 1) * SLOT)
        re, im = sent_ref[0, :, where].astype(f32), sent_ref[1, :, where].astype(f32)
        for k, value in enumerate((re * c + im * sn, im * c - re * sn)):
            for w in range(nw):
                for group in range(groups):
                    rows = []
                    for i in range(group * repeats, (group + 1) * repeats):
                        at = w * local_rows + i
                        rows.append(jnp.broadcast_to(value[at : at + 1], (peers, SLOT)))
                    turned_ref[k, w, group, :, where] = jnp.concatenate(rows, axis=0).astype(bf16)


def prepare(bands, sent, rows, nw):
    peers = 2 * rows
    fit = [n for n in range(1, rows + 1) if rows % n == 0 and n * peers % 16 == 0]
    repeats = fit[0] if fit else rows
    turned = (2, nw, rows // repeats, repeats * peers, KEPT)
    smem = pl.BlockSpec(memory_space=pltpu.SMEM)
    vmem = pl.BlockSpec(memory_space=pltpu.VMEM)
    return pl.pallas_call(
        functools.partial(prepare_kernel, peers),
        out_shape=jax.ShapeDtypeStruct(turned, bf16),
        in_specs=[smem, vmem],
        out_specs=vmem,
        compiler_params=pltpu.CompilerParams(vmem_limit_bytes=16 * 2**20),
        cost_estimate=pl.CostEstimate(flops=10**7, bytes_accessed=4 * 2**20, transcendentals=0),
        name="prepare",
    )(bands, sent)


def lag_kernel(bands_ref, base_ref, shift_ref, even_ref, odd_ref):
    place = lax.broadcasted_iota(jnp.int32, (SLOT, 1), 0)
    residue = RADIX * (place % FOLD) + place // FOLD
    for b in range(NBANDS):
        start = bands_ref[0, b]
        block = start // SLOT
        first = residue >= start % SLOT
        rows = [
            [shift_ref[k, pl.ds(block + step, 1), :] for step in range(2)] for k in range(2)
        ]
        c = jnp.where(first, rows[0][0], rows[0][1])
        s = jnp.where(first, rows[1][0], rows[1][1])
        weight = jnp.where(first & (residue + block * SLOT == 0), 0.5, 1.0)
        bc, bs = base_ref[0] * weight, base_ref[1] * weight
        even_ref[b * SLOT : (b + 1) * SLOT, :] = (bc * c - bs * s).astype(bf16)
        odd_ref[b * SLOT : (b + 1) * SLOT, :] = (bs * c + bc * s).astype(bf16)


def lag_tables(bands):
    base, shift = lag_constants()
    table = jax.ShapeDtypeStruct((KEPT, HALF), bf16)
    smem = pl.BlockSpec(memory_space=pltpu.SMEM)
    vmem = pl.BlockSpec(memory_space=pltpu.VMEM)
    return pl.pallas_call(
        lag_kernel,
        out_shape=[table, table],
        in_specs=[smem, vmem, vmem],
        out_specs=[vmem, vmem],
        compiler_params=pltpu.CompilerParams(vmem_limit_bytes=16 * 2**20),
        cost_estimate=pl.CostEstimate(flops=10**7, bytes_accessed=4 * 2**20, transcendentals=0),
        name="lag_tables",
    )(bands, base, shift)


def crossed(nw, rows, live, lanes, turned_ref, near_ref, swap_ref, cross_re, cross_im):
    _, _, groups, group_rows, _ = turned_ref.shape
    even_core = lax.rem(lax.axis_index("sta"), 2) == 0
    remote = []
    for k in range(2):
        near, swap = near_ref[k, :, lanes], swap_ref[k, :, lanes]
        by_core = [
            jnp.where(even_core, near, swap).astype(f32) * live,
            jnp.where(even_core, swap, near).astype(f32) * live,
        ]
        remote.append([])
        for w in range(nw):
            span = slice(w * rows, (w + 1) * rows)
            peers = jnp.concatenate([made[span] for made in by_core], axis=0)
            repeats = group_rows // (2 * rows)
            remote[k].append(jnp.concatenate([peers] * repeats, axis=0).astype(bf16))
    for row in range(0, group_rows, 16):
        end = min(row + 16, group_rows)
        there = [
            [remote[k][w][row:end] for w in range(nw)]
            for k in range(2)
        ]
        for group in range(groups):
            re, im = [], []
            for w in range(nw):
                lr = turned_ref[0, w, group, row:end, lanes]
                li = turned_ref[1, w, group, row:end, lanes]
                rr, ri = there[0][w], there[1][w]
                re.append(lr * rr + li * ri)
                im.append(li * rr - lr * ri)
            at = slice(group * group_rows + row, group * group_rows + end)
            cross_re[at, lanes] = (re[0] + re[1]) + (re[2] + re[3])
            cross_im[at, lanes] = (im[0] + im[1]) + (im[2] + im[3])


def mirrored(i, even, odd, value_ref):
    _, peers, _ = value_ref.shape
    backward = 127 - lax.broadcasted_iota(jnp.int32, (peers, 128), 1)
    middle = LAGS // 256
    for tile in range(HALF // 128):
        lanes = slice(tile * 128, (tile + 1) * 128)
        e, o = even[:, lanes], odd[:, lanes]
        after, before = (middle + tile) * 128, (middle - 1 - tile) * 128
        value_ref[i, :, after : after + 128] = e - o
        value_ref[i, :, before : before + 128] = jnp.take_along_axis(e + o, backward, axis=1)


def started(i, value_ref, out_ref, block, distance, sems):
    _, chips, _, _, _ = out_ref.shape
    chip = lax.rem(lax.axis_index("sta") // 2 + chips - distance, chips)
    copy = pltpu.make_async_copy(value_ref.at[i], out_ref.at[i, chip, :, block, :], sems.at[i])
    copy.start()
    return copy


def correlate_kernel(nw, batches, aliased, live_ref, turned_ref, even_ref, odd_ref, *rest):
    units = [unit for batch in batches for unit in batch]
    sources, rest = rest[: 2 * len(units)], rest[2 * len(units) :]
    if aliased:
        rest = rest[1:]
    out_ref, cross_re, cross_im, values, sems = rest
    rows = out_ref.shape[0]
    copies = []
    total = turned_ref.shape[2] * turned_ref.shape[3]
    peers = total // rows
    first = 0
    for batch in batches:
        for at in range(first, first + len(batch)):
            live = live_ref[:, units[at][0] : units[at][0] + 1].astype(f32)
            mine = pl.ds(at * total, total)
            for band in range(NBANDS):
                crossed(
                    nw,
                    rows,
                    live,
                    slice(band * SLOT, (band + 1) * SLOT),
                    turned_ref,
                    *sources[2 * at : 2 * at + 2],
                    cross_re.at[mine],
                    cross_im.at[mine],
                )
        span = slice(first * total, (first + len(batch)) * total)
        even = jnp.dot(cross_re[span, :], even_ref[...], preferred_element_type=f32)
        odd = jnp.dot(cross_im[span, :], odd_ref[...], preferred_element_type=f32)
        for at in range(first, first + len(batch)):
            block, distance = units[at]
            value_ref = values.at[at]
            for i in range(rows):
                row = (at - first) * total + i * peers
                mirrored(i, even[row : row + peers], odd[row : row + peers], value_ref)
                copies.append(started(i, value_ref, out_ref, block, distance, sems.at[at]))
        first += len(batch)
    for copy in copies:
        copy.wait()


def correlate(block_live, turned, tables, rows, chips, batches, sources, more=()):
    _, nw, groups, group_rows, _ = turned.shape
    total = groups * group_rows
    peers = 2 * rows
    units = sum(len(batch) for batch in batches)
    vmem = pl.BlockSpec(memory_space=pltpu.VMEM)
    output = pl.BlockSpec(memory_space=pl.ANY)
    operands = [block_live, turned, *tables, *sources]
    cross = pltpu.VMEM((units * total, KEPT), bf16)
    return pl.pallas_call(
        functools.partial(correlate_kernel, nw, batches, bool(more)),
        out_shape=jax.ShapeDtypeStruct((rows, chips, peers, OFFS, LAGS), f32),
        in_specs=[vmem] * len(operands) + [output] * len(more),
        out_specs=output,
        scratch_shapes=[
            cross,
            cross,
            pltpu.VMEM((units, rows, peers, LAGS), f32),
            pltpu.SemaphoreType.DMA((units, rows)),
        ],
        input_output_aliases={len(operands): 0} if more else {},
        compiler_params=pltpu.CompilerParams(vmem_limit_bytes=(24 if more else 32) * 2**20),
        cost_estimate=pl.CostEstimate(
            flops=4 * units * total * KEPT * HALF,
            bytes_accessed=8 * 2**20,
            transcendentals=0,
        ),
        name="last_part" if more else "middle_part",
    )(*operands, *more)


def next_group(block):
    axes = ("section", "grp")
    n = lax.axis_size(axes)
    return lax.ppermute(block, axes, [((i - 1) % n, i) for i in range(n)])


def swapped_core(block):
    n = lax.axis_size("sta")
    return lax.ppermute(block, "sta", [(i, i ^ 1) for i in range(n)])


def from_chip(block, distance):
    n = lax.axis_size("sta")
    return lax.ppermute(block, "sta", [(i, (i + 2 * distance) % n) for i in range(n)])


def tied(*values):
    return lax.optimization_barrier(values)


def body(records, fir_taps, band_bins, station_live, block_live):
    chips = lax.axis_size("sta") // 2
    ns, nw, nc, _ = records.shape
    rows = ns * nc
    bands = jnp.transpose(band_bins)
    sent = spectra(records, fir_taps, bands, station_live)
    turned = prepare(bands, sent, rows, nw)
    tables = lag_tables(bands)
    first, turned, *tables = tied(next_group(sent), turned, *tables)
    second = next_group(first)
    held = [first, swapped_core(first)]
    for d in range(1, chips):
        far = from_chip(first, d)
        held += [far, swapped_core(far)]
    far_second = [from_chip(second, d) for d in range(1, chips)]
    held += [second, swapped_core(second)]
    live = block_live.reshape(1, OFFS)
    batches = [[(0, d) for d in range(chips)], [(1, 0)]]
    result = correlate(live, turned, tables, rows, chips, batches, held)
    far_second, result = tied(far_second, result)
    for d in range(1, chips):
        held = [far_second[d - 1], swapped_core(far_second[d - 1])]
        result = correlate(live, turned, tables, rows, chips, [[(1, d)]], held, (result,))
    return result.reshape(-1, OFFS, LAGS)


def solution(mesh):
    in_specs = (
        P(("section", "grp", "sta"), None, None, None),
        P(),
        P(),
        P(("section", "grp", "sta")),
        P(("section", "grp")),
    )
    out_specs = P("sta", ("section", "grp"), None)
    return jax.shard_map(body, mesh=mesh, in_specs=in_specs, out_specs=out_specs, check_vma=False)
```

profile of v0, /device:TPU:0, one launch (start us, length us, event | category | flops | bytes accessed | tf_op | source)
XLA Modules:
  0.0 39.8 jit_solution(2263251686161384502)
XLA Ops:
  0.0 0.0 copy-start.3
  0.0 6.8 %spectra.1.sent_ref = bf16[2,48,1024]{2,1,0:T(8,128)(2,1)} custom-call(bf16[12,4,16384]{2,1,0:T(4,128)(2,1)} %bitcast.13, f32[1,64]{1,0:T(1,128)} %bitcast.14, s32[2,4]{1,0:T(2,128)} %bitcast.8, s32[1,4]{1,0:T(1,128)} %bitcast.15, bf16[2,2,512,128]{3,2,1,0:T(8,128)(2,1)} %constant.14.clone.table_hbm, f32[2,16,256]{2,1,0:T(8,128)} %constant.15.clone.twiddle_hbm, ...), custom_call_target="tpu_custom_call" | custom-call | flops 3000000000 | bytes 5242880 | tf_op jit(solution)/shard_map/spectra/pallas_call | solution.py:305
  6.8 0.0 copy-start
  6.9 3.1 %collective-permute-start = (bf16[2,48,1024]{2,1,0:T(8,128)(2,1)}, bf16[2,48,1024]{2,1,0:T(8,128)(2,1)S(1)}, u32[]{:S(2)}, u32[]{:S(2)}) collective-permute-start(bf16[2,48,1024]{2,1,0:T(8,128)(2,1)} %spectra.1.sent_ref), channel_id=1, source_target_pairs={{28,0},{0,4},{4,8},{8,12},{12,16},{16,20},{20,24},{24,28},{29,1},{... | collective-permute-start | bytes 589832 | tf_op jit(solution)/shard_map/ppermute | solution.py:530
  9.9 0.0 copy-done.3
  9.9 0.0 copy-start.1
  9.9 1.0 %copy-done.1 = bf16[2,48,1024]{2,1,0:T(8,128)(2,1)S(1)} copy-done((bf16[2,48,1024]{2,1,0:T(8,128)(2,1)S(1)}, bf16[2,48,1024]{2,1,0:T(8,128)(2,1)}, u32[]{:S(2)}) %copy-start.1) | copy-done | bytes 196632
  10.9 0.0 copy-start.2
  10.9 0.0 copy-start.4
  10.9 1.3 %prepare.1.turned_ref = bf16[2,4,6,48,1024]{4,3,2,1,0:T(8,128)(2,1)S(1)} custom-call(s32[2,4]{1,0:T(2,128)S(1)} %bitcast.9, bf16[2,48,1024]{2,1,0:T(8,128)(2,1)S(1)} %copy-done.1), custom_call_target="tpu_custom_call" | custom-call | flops 10000000 | bytes 4194304 | tf_op jit(solution)/shard_map/prepare/pallas_call | solution.py:355
  12.2 0.0 copy-done
  12.2 0.0 copy-done.2
  12.2 1.6 %lag_tables.1 = (bf16[1024,512]{1,0:T(8,128)(2,1)S(1)}, bf16[1024,512]{1,0:T(8,128)(2,1)S(1)}) custom-call(s32[2,4]{1,0:T(2,128)S(1)} %bitcast.10, f32[2,256,512]{2,1,0:T(8,128)S(1)} %copy-done, f32[2,16,512]{2,1,0:T(8,128)S(1)} %copy-done.2), custom_call_target="tpu_custom_call" | custom-call | flops 10000000 | bytes 4194304 | tf_op jit(solution)/shard_map/lag_tables/pallas_call | solution.py:389
  13.9 4.2 %collective-permute-done.rest_0_ = bf16[2,48,1024]{2,1,0:T(8,128)(2,1)S(1)} collective-permute-done((bf16[2,48,1024]{2,1,0:T(8,128)(2,1)}, bf16[2,48,1024]{2,1,0:T(8,128)(2,1)S(1)}, u32[]{:S(2)}, u32[]{:S(2)}) %collective-permute-start) | collective-permute-done | bytes 196640 | tf_op jit(solution)/shard_map/ppermute | solution.py:530
  18.0 1.5 %collective-permute-start.4 = (bf16[2,48,1024]{2,1,0:T(8,128)(2,1)S(1)}, bf16[2,48,1024]{2,1,0:T(8,128)(2,1)S(1)}, u32[]{:S(2)}, u32[]{:S(2)}) collective-permute-start(bf16[2,48,1024]{2,1,0:T(8,128)(2,1)S(1)} %collective-permute-done.rest_0_), channel_id=1, source_target_pairs={{0,2},{1,3},{2,0},{3,1},{4,6},{5,7},{6,4},{7,5},{8,10},{9,11},{10,... | collective-permute-start | bytes 589832 | tf_op jit(solution)/shard_map/ppermute | solution.py:540
  19.5 0.0 collective-permute-start.1
  19.5 0.0 collective-permute-start.3
  19.5 4.6 %collective-permute-done.4.rest_2_ = bf16[2,48,1024]{2,1,0:T(8,128)(2,1)S(1)} collective-permute-done((bf16[2,48,1024]{2,1,0:T(8,128)(2,1)S(1)}, bf16[2,48,1024]{2,1,0:T(8,128)(2,1)S(1)}, u32[]{:S(2)}, u32[]{:S(2)}) %collective-permute-start.4) | collective-permute-done | bytes 196640 | tf_op jit(solution)/shard_map/ppermute | solution.py:540
  24.1 0.0 collective-permute-start.5
  24.1 3.8 %collective-permute-done.1.rest_4_ = bf16[2,48,1024]{2,1,0:T(8,128)(2,1)S(1)} collective-permute-done((bf16[2,48,1024]{2,1,0:T(8,128)(2,1)S(1)}, bf16[2,48,1024]{2,1,0:T(8,128)(2,1)S(1)}, u32[]{:S(2)}, u32[]{:S(2)}) %collective-permute-start.1) | collective-permute-done | bytes 196640 | tf_op jit(solution)/shard_map/ppermute | solution.py:530
  27.9 0.0 collective-permute-start.6
  27.9 0.7 %collective-permute-start.2 = (bf16[2,48,1024]{2,1,0:T(8,128)(2,1)S(1)}, bf16[2,48,1024]{2,1,0:T(8,128)(2,1)S(1)}, u32[]{:S(2)}, u32[]{:S(2)}) collective-permute-start(bf16[2,48,1024]{2,1,0:T(8,128)(2,1)S(1)} %collective-permute-done.1.rest_4_), channel_id=1, source_target_pairs={{0,2},{1,3},{2,0},{3,1},{4,6},{5,7},{6,4},{7,5},{8,10},{9,11},{10,... | collective-permute-start | bytes 589832 | tf_op jit(solution)/shard_map/ppermute | solution.py:540
  28.6 0.0 collective-permute-done.3.rest_1_
  28.6 0.0 collective-permute-done.5.rest_3_
  28.6 0.8 %collective-permute-done.6.rest_5_ = bf16[2,48,1024]{2,1,0:T(8,128)(2,1)S(1)} collective-permute-done((bf16[2,48,1024]{2,1,0:T(8,128)(2,1)S(1)}, bf16[2,48,1024]{2,1,0:T(8,128)(2,1)S(1)}, u32[]{:S(2)}, u32[]{:S(2)}) %collective-permute-start.6) | collective-permute-done | bytes 196640 | tf_op jit(solution)/shard_map/ppermute | solution.py:535
  29.3 0.0 copy-done.4
  29.3 6.1 %middle_part.1.rest_2_ = f32[12,2,24,2,1024]{4,3,2,1,0:T(2,128)} custom-call(s32[1,2]{1,0:T(1,128)S(1)} %bitcast.11, bf16[2,4,6,48,1024]{4,3,2,1,0:T(8,128)(2,1)S(1)} %prepare.1.turned_ref, bf16[1024,512]{1,0:T(8,128)(2,1)S(1)} %get-tuple-element.16.even_ref, bf16[1024,512]{1,0:T(8,128)(2,1)S(1)} %get-tuple-element.17.odd_ref, ...), custom_call_target="tpu_custom_call" | custom-call | flops 1811939328 | bytes 8388608 | tf_op jit(solution)/shard_map/middle_part/pallas_call | solution.py:505
  35.4 0.0 collective-permute-done.2.rest_0_
  35.4 0.2 collective-permute-start.7
  35.6 1.3 %collective-permute-done.7.rest_1_ = bf16[2,48,1024]{2,1,0:T(8,128)(2,1)S(1)} collective-permute-done((bf16[2,48,1024]{2,1,0:T(8,128)(2,1)S(1)}, bf16[2,48,1024]{2,1,0:T(8,128)(2,1)S(1)}, u32[]{:S(2)}, u32[]{:S(2)}) %collective-permute-start.7) | collective-permute-done | bytes 196640 | tf_op jit(solution)/shard_map/ppermute | solution.py:535
  36.9 2.7 %last_part.1 = f32[12,2,24,2,1024]{4,3,2,1,0:T(2,128)} custom-call(s32[1,2]{1,0:T(1,128)S(1)} %bitcast.12, bf16[2,4,6,48,1024]{4,3,2,1,0:T(8,128)(2,1)S(1)} %prepare.1.turned_ref, bf16[1024,512]{1,0:T(8,128)(2,1)S(1)} %get-tuple-element.16.even_ref, bf16[1024,512]{1,0:T(8,128)(2,1)S(1)} %get-tuple-element.17.odd_ref, ...), custom_call_target="tpu_custom_call", output_to_operand_aliasing={{}: (6, {})} | custom-call | flops 603979776 | bytes 8388608 | tf_op jit(solution)/shard_map/last_part/pallas_call | solution.py:505
Async XLA Ops:
  0.0 9.9 %copy-start.3 = (s32[4,2]{0,1:T(2,128)S(1)}, s32[4,2]{0,1:T(2,128)}, u32[]{:S(2)}) copy-start(s32[4,2]{0,1:T(2,128)} %param.14) | copy-start | bytes 100
  6.8 5.4 %copy-start = (f32[2,256,512]{2,1,0:T(8,128)S(1)}, f32[2,256,512]{2,1,0:T(8,128)}, u32[]{:S(2)}) copy-start(f32[2,256,512]{2,1,0:T(8,128)} %constant.19.clone.base_ref) | copy-start | bytes 3145732
  6.9 11.2 %collective-permute-start = (bf16[2,48,1024]{2,1,0:T(8,128)(2,1)}, bf16[2,48,1024]{2,1,0:T(8,128)(2,1)S(1)}, u32[]{:S(2)}, u32[]{:S(2)}) collective-permute-start(bf16[2,48,1024]{2,1,0:T(8,128)(2,1)} %spectra.1.sent_ref), channel_id=1, source_target_pairs={{28,0},{0,4},{4,8},{8,12},{12,16},{16,20},{20,24},{24,28},{29,1},{... | collective-permute-start | bytes 589832 | tf_op jit(solution)/shard_map/ppermute | solution.py:530
  9.9 1.0 %copy-start.1 = (bf16[2,48,1024]{2,1,0:T(8,128)(2,1)S(1)}, bf16[2,48,1024]{2,1,0:T(8,128)(2,1)}, u32[]{:S(2)}) copy-start(bf16[2,48,1024]{2,1,0:T(8,128)(2,1)} %spectra.1.sent_ref) | copy-start | bytes 589828
  10.9 1.3 %copy-start.2 = (f32[2,16,512]{2,1,0:T(8,128)S(1)}, f32[2,16,512]{2,1,0:T(8,128)}, u32[]{:S(2)}) copy-start(f32[2,16,512]{2,1,0:T(8,128)} %constant.20.clone.shift_ref) | copy-start | bytes 196612
  10.9 18.4 %copy-start.4 = (s32[2]{0:T(128)S(1)}, s32[2]{0:T(128)}, u32[]{:S(2)}) copy-start(s32[2]{0:T(128)} %param.16) | copy-start | bytes 28
  18.0 6.1 %collective-permute-start.4 = (bf16[2,48,1024]{2,1,0:T(8,128)(2,1)S(1)}, bf16[2,48,1024]{2,1,0:T(8,128)(2,1)S(1)}, u32[]{:S(2)}, u32[]{:S(2)}) collective-permute-start(bf16[2,48,1024]{2,1,0:T(8,128)(2,1)S(1)} %collective-permute-done.rest_0_), channel_id=1, source_target_pairs={{0,2},{1,3},{2,0},{3,1},{4,6},{5,7},{6,4},{7,5},{8,10},{9,11},{10,... | collective-permute-start | bytes 589832 | tf_op jit(solution)/shard_map/ppermute | solution.py:540
  19.5 8.4 %collective-permute-start.1 = (bf16[2,48,1024]{2,1,0:T(8,128)(2,1)S(1)}, bf16[2,48,1024]{2,1,0:T(8,128)(2,1)S(1)}, u32[]{:S(2)}, u32[]{:S(2)}) collective-permute-start(bf16[2,48,1024]{2,1,0:T(8,128)(2,1)S(1)} %collective-permute-done.rest_0_), channel_id=1, source_target_pairs={{28,0},{0,4},{4,8},{8,12},{12,16},{16,20},{20,24},{24,28},{29,1},{... | collective-permute-start | bytes 589832 | tf_op jit(solution)/shard_map/ppermute | solution.py:530
  19.5 9.0 %collective-permute-start.3 = (bf16[2,48,1024]{2,1,0:T(8,128)(2,1)S(1)}, bf16[2,48,1024]{2,1,0:T(8,128)(2,1)S(1)}, u32[]{:S(2)}, u32[]{:S(2)}) collective-permute-start(bf16[2,48,1024]{2,1,0:T(8,128)(2,1)S(1)} %collective-permute-done.rest_0_), channel_id=1, source_target_pairs={{0,1},{1,0},{2,3},{3,2},{4,5},{5,4},{6,7},{7,6},{8,9},{9,8},{10,11... | collective-permute-start | bytes 589832 | tf_op jit(solution)/shard_map/ppermute | solution.py:535
  24.1 4.5 %collective-permute-start.5 = (bf16[2,48,1024]{2,1,0:T(8,128)(2,1)S(1)}, bf16[2,48,1024]{2,1,0:T(8,128)(2,1)S(1)}, u32[]{:S(2)}, u32[]{:S(2)}) collective-permute-start(bf16[2,48,1024]{2,1,0:T(8,128)(2,1)S(1)} %collective-permute-done.4.rest_2_), channel_id=1, source_target_pairs={{0,1},{1,0},{2,3},{3,2},{4,5},{5,4},{6,7},{7,6},{8,9},{9,8},{10,11... | collective-permute-start | bytes 589832 | tf_op jit(solution)/shard_map/ppermute | solution.py:535
  27.9 1.4 %collective-permute-start.6 = (bf16[2,48,1024]{2,1,0:T(8,128)(2,1)S(1)}, bf16[2,48,1024]{2,1,0:T(8,128)(2,1)S(1)}, u32[]{:S(2)}, u32[]{:S(2)}) collective-permute-start(bf16[2,48,1024]{2,1,0:T(8,128)(2,1)S(1)} %collective-permute-done.1.rest_4_), channel_id=1, source_target_pairs={{0,1},{1,0},{2,3},{3,2},{4,5},{5,4},{6,7},{7,6},{8,9},{9,8},{10,11... | collective-permute-start | bytes 589832 | tf_op jit(solution)/shard_map/ppermute | solution.py:535
  27.9 7.5 %collective-permute-start.2 = (bf16[2,48,1024]{2,1,0:T(8,128)(2,1)S(1)}, bf16[2,48,1024]{2,1,0:T(8,128)(2,1)S(1)}, u32[]{:S(2)}, u32[]{:S(2)}) collective-permute-start(bf16[2,48,1024]{2,1,0:T(8,128)(2,1)S(1)} %collective-permute-done.1.rest_4_), channel_id=1, source_target_pairs={{0,2},{1,3},{2,0},{3,1},{4,6},{5,7},{6,4},{7,5},{8,10},{9,11},{10,... | collective-permute-start | bytes 589832 | tf_op jit(solution)/shard_map/ppermute | solution.py:540
  35.4 1.5 %collective-permute-start.7 = (bf16[2,48,1024]{2,1,0:T(8,128)(2,1)S(1)}, bf16[2,48,1024]{2,1,0:T(8,128)(2,1)S(1)}, u32[]{:S(2)}, u32[]{:S(2)}) collective-permute-start(bf16[2,48,1024]{2,1,0:T(8,128)(2,1)S(1)} %collective-permute-done.2.rest_0_), channel_id=1, source_target_pairs={{0,1},{1,0},{2,3},{3,2},{4,5},{5,4},{6,7},{7,6},{8,9},{9,8},{10,11... | collective-permute-start | bytes 589832 | tf_op jit(solution)/shard_map/ppermute | solution.py:535
where the time goes:
time: 39.9 us; the launch traced here: 39.8 us
  Pallas kernels  18.5 us (46%)
  waiting for transfers between devices  14.6 us (37%)
  starting transfers between devices  5.45 us (14%)
  local copies, waits for them, and re-layouts  0.98 us (2%)
    pallas_call x2, Pallas kernels, correlate(): pl.pallas_call(functools.partial(correlate_kernel, nw, batches, bool(more...  8.74 us
    ppermute x2, waiting for transfers between devices, next_group(): return lax.ppermute(block, axes, [((i - 1) % n, i) for i in range(n)])  7.94 us
    pallas_call x1, Pallas kernels, spectra(): pl.pallas_call(spectra_kernel, out_shape=jax.ShapeDtypeStruct((2, nw * gr...  6.84 us
    ppermute x2, waiting for transfers between devices, from_chip(): lax.ppermute(block, 'sta', [(i, (i + 2 * distance) % n) for i in range(n)])  4.59 us
    ppermute x2, starting transfers between devices, next_group(): return lax.ppermute(block, axes, [((i - 1) % n, i) for i in range(n)])  3.08 us
    ppermute x2, starting transfers between devices, from_chip(): lax.ppermute(block, 'sta', [(i, (i + 2 * distance) % n) for i in range(n)])  2.16 us
    ppermute x4, waiting for transfers between devices, swapped_core(): return lax.ppermute(block, 'sta', [(i, i ^ 1) for i in range(n)])  2.07 us
    pallas_call x1, Pallas kernels, lag_tables(): pl.pallas_call(lag_kernel, out_shape=[table, table], in_specs=[smem, vmem...  1.63 us
  transfers between devices with their start and end apart: 8, of which 5 were waited for; matrix products, arithmetic and copies ran while one was open for 0% of the time, Pallas kernels for 23%

commit v1 on v0

--- a/solution.py
+++ b/solution.py
@@ -47,12 +47,6 @@
     return jnp.concatenate([ref[i] for i in range(ref.shape[0])], axis=1)
 
 
-def split_const(table):
-    high = table.astype(np.float32).astype(bf16)
-    low = (table - high.astype(np.float64)).astype(np.float32).astype(bf16)
-    return high, low
-
-
 def compact_order():
     place = np.arange(SLOT)
     return RADIX * (place % FOLD) + place // FOLD
@@ -66,7 +60,6 @@
     table = np.concatenate(
         [np.concatenate([cos, -sin], axis=1), np.concatenate([sin, cos], axis=1)], axis=0
     )
-    high, low = split_const(table)
     h = np.arange(RADIX)
     turn = 2.0 * np.pi * (h[:, None] * inner[None, :]) / NT
     twiddle = np.stack([np.cos(turn), -np.sin(turn)]).astype(np.float32)
@@ -76,7 +69,7 @@
     for step in range(RADIX):
         fold[step, np.arange(BIG), FOLD * step + np.arange(BIG) % FOLD] = 1.0
     fold = by_tile(fold.reshape(BINS, SLOT).astype(bf16))
-    return np.stack([by_tile(high), by_tile(low)]), twiddle, by_tile(place.astype(bf16)), fold
+    return by_tile(table.astype(np.float32).astype(bf16)), twiddle, by_tile(place.astype(bf16)), fold
 
 
 def lag_constants():
@@ -142,8 +135,7 @@
     place_ref,
     fold_ref,
     order_ref,
-    u_high,
-    u_low,
+    turned,
     kept,
     sems,
 ):
@@ -213,18 +205,11 @@
                 ur, ui = yr * c - yi * sn, yr * sn + yi * c
             for k, u in enumerate((ur, ui)):
                 where = slice(k * INNER, (k + 1) * INNER)
-                top = u.astype(bf16)
-                u_high[h * ch + at : h * ch + at + 16, where] = top
-                u_low[h * ch + at : h * ch + at + 16, where] = (u - top.astype(f32)).astype(bf16)
+                turned[h * ch + at : h * ch + at + 16, where] = u.astype(bf16)
 
     for copy in copies[3 + PIECES :]:
         copy.wait()
-    table_high, table_low = joined(table_ref.at[0]), joined(table_ref.at[1])
-    spectrum = (
-        jnp.dot(u_high[...], table_high, preferred_element_type=f32)
-        + jnp.dot(u_low[...], table_high, preferred_element_type=f32)
-        + jnp.dot(u_high[...], table_low, preferred_element_type=f32)
-    )
+    spectrum = jnp.dot(turned[...], joined(table_ref), preferred_element_type=f32)
 
     row = lax.broadcasted_iota(jnp.int32, (ch, 1), 0)
     station = row // 12
@@ -309,7 +294,6 @@
         out_specs=pl.BlockSpec(memory_space=pltpu.VMEM),
         scratch_shapes=[pltpu.VMEM(o.shape, o.dtype) for o in operands]
         + [
-            pltpu.VMEM((RADIX * ch, 2 * INNER), bf16),
             pltpu.VMEM((RADIX * ch, 2 * INNER), bf16),
             pltpu.VMEM((2 * NBANDS * ch, BINS), bf16),
             pltpu.SemaphoreType.DMA((len(operands) - 1 + PIECES,)),
@@ -452,75 +436,89 @@
     return copy
 
 
-def correlate_kernel(nw, batches, aliased, live_ref, turned_ref, even_ref, odd_ref, *rest):
-    units = [unit for batch in batches for unit in batch]
+def correlate_kernel(nw, units, aliased, live_ref, turned_ref, even_ref, odd_ref, *rest):
     sources, rest = rest[: 2 * len(units)], rest[2 * len(units) :]
     if aliased:
         rest = rest[1:]
     out_ref, cross_re, cross_im, values, sems = rest
     rows = out_ref.shape[0]
-    copies = []
     total = turned_ref.shape[2] * turned_ref.shape[3]
     peers = total // rows
-    first = 0
-    for batch in batches:
-        for at in range(first, first + len(batch)):
-            live = live_ref[:, units[at][0] : units[at][0] + 1].astype(f32)
-            mine = pl.ds(at * total, total)
-            for band in range(NBANDS):
-                crossed(
-                    nw,
-                    rows,
-                    live,
-                    slice(band * SLOT, (band + 1) * SLOT),
-                    turned_ref,
-                    *sources[2 * at : 2 * at + 2],
-                    cross_re.at[mine],
-                    cross_im.at[mine],
-                )
-        span = slice(first * total, (first + len(batch)) * total)
-        even = jnp.dot(cross_re[span, :], even_ref[...], preferred_element_type=f32)
-        odd = jnp.dot(cross_im[span, :], odd_ref[...], preferred_element_type=f32)
-        for at in range(first, first + len(batch)):
-            block, distance = units[at]
-            value_ref = values.at[at]
-            for i in range(rows):
-                row = (at - first) * total + i * peers
-                mirrored(i, even[row : row + peers], odd[row : row + peers], value_ref)
-                copies.append(started(i, value_ref, out_ref, block, distance, sems.at[at]))
-        first += len(batch)
+    bands = [slice(band * SLOT, (band + 1) * SLOT) for band in range(NBANDS)]
+    copies = []
+
+    def cross(at, band):
+        crossed(
+            nw,
+            rows,
+            live_ref[:, units[at][0] : units[at][0] + 1].astype(f32),
+            bands[band],
+            turned_ref,
+            *sources[2 * at : 2 * at + 2],
+            cross_re.at[at],
+            cross_im.at[at],
+        )
+
+    def summed(at, lanes):
+        even = jnp.dot(cross_re[at, :, lanes], even_ref[lanes, :], preferred_element_type=f32)
+        odd = jnp.dot(cross_im[at, :, lanes], odd_ref[lanes, :], preferred_element_type=f32)
+        return even, odd
+
+    def finished(at, even, odd):
+        block, distance = units[at]
+        for i in range(rows):
+            span = slice(i * peers, (i + 1) * peers)
+            mirrored(i, even[span], odd[span], values.at[at])
+            copies.append(started(i, values.at[at], out_ref, block, distance, sems.at[at]))
+
+    if len(units) == 1:
+        half = NBANDS // 2
+        parts = []
+        for first in (0, half):
+            for band in range(first, first + half):
+                cross(0, band)
+            parts.append(summed(0, slice(first * SLOT, (first + half) * SLOT)))
+        (even, odd), (more_even, more_odd) = parts
+        finished(0, even + more_even, odd + more_odd)
+    else:
+        for at in range(len(units) + 1):
+            if at < len(units):
+                for band in range(NBANDS):
+                    cross(at, band)
+            if at:
+                finished(at - 1, *summed(at - 1, slice(0, KEPT)))
     for copy in copies:
         copy.wait()
 
 
-def correlate(block_live, turned, tables, rows, chips, batches, sources, more=()):
+def correlate(block_live, turned, tables, rows, chips, units, sources, more=()):
     _, nw, groups, group_rows, _ = turned.shape
     total = groups * group_rows
     peers = 2 * rows
-    units = sum(len(batch) for batch in batches)
+    n = len(units)
     vmem = pl.BlockSpec(memory_space=pltpu.VMEM)
     output = pl.BlockSpec(memory_space=pl.ANY)
     operands = [block_live, turned, *tables, *sources]
-    cross = pltpu.VMEM((units * total, KEPT), bf16)
+    cross = pltpu.VMEM((n, total, KEPT), bf16)
     return pl.pallas_call(
-        functools.partial(correlate_kernel, nw, batches, bool(more)),
+        functools.partial(correlate_kernel, nw, units, bool(more)),
         out_shape=jax.ShapeDtypeStruct((rows, chips, peers, OFFS, LAGS), f32),
         in_specs=[vmem] * len(operands) + [output] * len(more),
         out_specs=output,
         scratch_shapes=[
             cross,
             cross,
-            pltpu.VMEM((units, rows, peers, LAGS), f32),
-            pltpu.SemaphoreType.DMA((units, rows)),
+            pltpu.VMEM((n, rows, peers, LAGS), f32),
+            pltpu.SemaphoreType.DMA((n, rows)),
         ],
         input_output_aliases={len(operands): 0} if more else {},
         compiler_params=pltpu.CompilerParams(vmem_limit_bytes=(24 if more else 32) * 2**20),
         cost_estimate=pl.CostEstimate(
-            flops=4 * units * total * KEPT * HALF,
+            flops=4 * n * total * KEPT * HALF,
             bytes_accessed=8 * 2**20,
             transcendentals=0,
         ),
-        name="last_part" if more else "middle_part",
+        name="block_rows",
     )(*operands, *more)
 
 
@@ -554,19 +552,25 @@
     tables = lag_tables(bands)
     first, turned, *tables = tied(next_group(sent), turned, *tables)
     second = next_group(first)
-    held = [first, swapped_core(first)]
-    for d in range(1, chips):
-        far = from_chip(first, d)
-        held += [far, swapped_core(far)]
+    far = [from_chip(first, d) for d in range(1, chips)]
+    near_swap = swapped_core(first)
+    far, second = tied(far, second)
+    held = [first, near_swap]
+    for block in far:
+        held += [block, swapped_core(block)]
     far_second = [from_chip(second, d) for d in range(1, chips)]
-    held += [second, swapped_core(second)]
+    near_swap = swapped_core(second)
     live = block_live.reshape(1, OFFS)
-    batches = [[(0, d) for d in range(chips)], [(1, 0)]]
-    result = correlate(live, turned, tables, rows, chips, batches, held)
+
+    def written(units, held, *more):
+        return correlate(live, turned, tables, rows, chips, units, held, more)
+
+    units = [(0, d) for d in range(chips)] + [(1, 0)]
+    result = written(units, held + [second, near_swap])
     far_second, result = tied(far_second, result)
     for d in range(1, chips):
-        held = [far_second[d - 1], swapped_core(far_second[d - 1])]
-        result = correlate(live, turned, tables, rows, chips, [[(1, d)]], held, (result,))
+        far = far_second[d - 1]
+        result = written([(1, d)], [far, swapped_core(far)], result)
     return result.reshape(-1, OFFS, LAGS)
 
 

time: 39.9 us -> 38.3 us (0.960)
  waiting for transfers between devices: 14.6 us -> 12.8 us
  starting transfers between devices: 5.45 us -> 6.58 us
  Pallas kernels: 18.5 us -> 17.7 us
    ppermute x2, waiting for transfers between devices: 4.59 us -> 0.01 us  [from_chip(): lax.ppermute(block, 'sta', [(i, (i + 2 * distance) % n) for i in range(n)])]
    ppermute x2, waiting for transfers between devices: 7.94 us -> 11.5 us  [next_group(): return lax.ppermute(block, axes, [((i - 1) % n, i) for i in range(n)])]
    pallas_call x1, Pallas kernels: 6.84 us -> 5.91 us  [spectra(): pl.pallas_call(spectra_kernel, out_shape=jax.ShapeDtypeStruct((2, nw * gr...]
    ppermute x4, waiting for transfers between devices: 2.07 us -> 1.34 us  [swapped_core(): return lax.ppermute(block, 'sta', [(i, i ^ 1) for i in range(n)])]
    ppermute x2, starting transfers between devices: 2.16 us -> 2.81 us  [from_chip(): lax.ppermute(block, 'sta', [(i, (i + 2 * distance) % n) for i in range(n)])]
    ppermute x4, starting transfers between devices: 0.21 us -> 0.69 us  [swapped_core(): return lax.ppermute(block, 'sta', [(i, i ^ 1) for i in range(n)])]
  transfers between devices with their start and end apart: 8 -> 8, of which waited for: 5 -> 3; matrix products, arithmetic and copies ran while one was open for 0% -> 0% of each run, Pallas kernels for 23% -> 24%
where the time goes in v1:
time: 38.3 us; the launch traced here: 38.1 us
  Pallas kernels  17.7 us (46%)
  waiting for transfers between devices  12.8 us (33%)
  starting transfers between devices  6.58 us (17%)
  local copies, waits for them, and re-layouts  0.98 us (3%)
    ppermute x2, waiting for transfers between devices, next_group(): return lax.ppermute(block, axes, [((i - 1) % n, i) for i in range(n)])  11.5 us
    pallas_call x2, Pallas kernels, correlate(): pl.pallas_call(functools.partial(correlate_kernel, nw, units, bool(more))...  8.84 us
    pallas_call x1, Pallas kernels, spectra(): pl.pallas_call(spectra_kernel, out_shape=jax.ShapeDtypeStruct((2, nw * gr...  5.91 us
    ppermute x2, starting transfers between devices, next_group(): return lax.ppermute(block, axes, [((i - 1) % n, i) for i in range(n)])  3.08 us
    ppermute x2, starting transfers between devices, from_chip(): lax.ppermute(block, 'sta', [(i, (i + 2 * distance) % n) for i in range(n)])  2.81 us
    pallas_call x1, Pallas kernels, lag_tables(): pl.pallas_call(lag_kernel, out_shape=[table, table], in_specs=[smem, vmem...  1.63 us
    ppermute x4, waiting for transfers between devices, swapped_core(): return lax.ppermute(block, 'sta', [(i, i ^ 1) for i in range(n)])  1.34 us
    pallas_call x1, Pallas kernels, prepare(): pl.pallas_call(functools.partial(prepare_kernel, peers), out_shape=jax.Sh...  1.29 us
  transfers between devices with their start and end apart: 8, of which 3 were waited for; matrix products, arithmetic and copies ran while one was open for 0% of the time, Pallas kernels for 24%

profile of v1, /device:TPU:0, one launch (start us, length us, event | category | flops | bytes accessed | tf_op | source)
XLA Modules:
  0.0 38.1 jit_solution(4404773220171471162)
XLA Ops:
  0.0 0.0 copy-start.3
  0.0 5.9 %spectra.1.sent_ref = bf16[2,48,1024]{2,1,0:T(8,128)(2,1)} custom-call(bf16[12,4,16384]{2,1,0:T(4,128)(2,1)} %bitcast.13, f32[1,64]{1,0:T(1,128)} %bitcast.14, s32[2,4]{1,0:T(2,128)} %bitcast.8, s32[1,4]{1,0:T(1,128)} %bitcast.15, bf16[2,512,128]{2,1,0:T(8,128)(2,1)} %constant.14.clone.table_hbm, f32[2,16,256]{2,1,0:T(8,128)} %constant.15.clone.twiddle_hbm, ...), custom_call_target="tpu_custom_call" | custom-call | flops 3000000000 | bytes 5242880 | tf_op jit(solution)/shard_map/spectra/pallas_call | solution.py:290
  5.9 0.0 copy-start
  5.9 3.1 %collective-permute-start = (bf16[2,48,1024]{2,1,0:T(8,128)(2,1)}, bf16[2,48,1024]{2,1,0:T(8,128)(2,1)S(1)}, u32[]{:S(2)}, u32[]{:S(2)}) collective-permute-start(bf16[2,48,1024]{2,1,0:T(8,128)(2,1)} %spectra.1.sent_ref), channel_id=1, source_target_pairs={{28,0},{0,4},{4,8},{8,12},{12,16},{16,20},{20,24},{24,28},{29,1},{... | collective-permute-start | bytes 589832 | tf_op jit(solution)/shard_map/ppermute | solution.py:528
  9.0 0.0 copy-done.3
  9.0 0.0 copy-start.1
  9.0 1.0 %copy-done.1 = bf16[2,48,1024]{2,1,0:T(8,128)(2,1)S(1)} copy-done((bf16[2,48,1024]{2,1,0:T(8,128)(2,1)S(1)}, bf16[2,48,1024]{2,1,0:T(8,128)(2,1)}, u32[]{:S(2)}) %copy-start.1) | copy-done | bytes 196632
  10.0 0.0 copy-start.2
  10.0 0.0 copy-start.4
  10.0 1.3 %prepare.1.turned_ref = bf16[2,4,6,48,1024]{4,3,2,1,0:T(8,128)(2,1)S(1)} custom-call(s32[2,4]{1,0:T(2,128)S(1)} %bitcast.9, bf16[2,48,1024]{2,1,0:T(8,128)(2,1)S(1)} %copy-done.1), custom_call_target="tpu_custom_call" | custom-call | flops 10000000 | bytes 4194304 | tf_op jit(solution)/shard_map/prepare/pallas_call | solution.py:339
  11.3 0.0 copy-done
  11.3 0.0 copy-done.2
  11.3 1.6 %lag_tables.1 = (bf16[1024,512]{1,0:T(8,128)(2,1)S(1)}, bf16[1024,512]{1,0:T(8,128)(2,1)S(1)}) custom-call(s32[2,4]{1,0:T(2,128)S(1)} %bitcast.10, f32[2,256,512]{2,1,0:T(8,128)S(1)} %copy-done, f32[2,16,512]{2,1,0:T(8,128)S(1)} %copy-done.2), custom_call_target="tpu_custom_call" | custom-call | flops 10000000 | bytes 4194304 | tf_op jit(solution)/shard_map/lag_tables/pallas_call | solution.py:373
  12.9 4.2 %collective-permute-done.rest_0_ = bf16[2,48,1024]{2,1,0:T(8,128)(2,1)S(1)} collective-permute-done((bf16[2,48,1024]{2,1,0:T(8,128)(2,1)}, bf16[2,48,1024]{2,1,0:T(8,128)(2,1)S(1)}, u32[]{:S(2)}, u32[]{:S(2)}) %collective-permute-start) | collective-permute-done | bytes 196640 | tf_op jit(solution)/shard_map/ppermute | solution.py:528
  17.1 0.0 collective-permute-start.2
  17.1 1.5 %collective-permute-start.1 = (bf16[2,48,1024]{2,1,0:T(8,128)(2,1)S(1)}, bf16[2,48,1024]{2,1,0:T(8,128)(2,1)S(1)}, u32[]{:S(2)}, u32[]{:S(2)}) collective-permute-start(bf16[2,48,1024]{2,1,0:T(8,128)(2,1)S(1)} %collective-permute-done.rest_0_), channel_id=1, source_target_pairs={{0,2},{1,3},{2,0},{3,1},{4,6},{5,7},{6,4},{7,5},{8,10},{9,11},{10,... | collective-permute-start | bytes 589832 | tf_op jit(solution)/shard_map/ppermute | solution.py:538
  18.6 0.0 collective-permute-start.4
  18.6 7.3 %collective-permute-done.2.rest_4_ = bf16[2,48,1024]{2,1,0:T(8,128)(2,1)S(1)} collective-permute-done((bf16[2,48,1024]{2,1,0:T(8,128)(2,1)S(1)}, bf16[2,48,1024]{2,1,0:T(8,128)(2,1)S(1)}, u32[]{:S(2)}, u32[]{:S(2)}) %collective-permute-start.2) | collective-permute-done | bytes 196640 | tf_op jit(solution)/shard_map/ppermute | solution.py:528
  25.9 0.0 collective-permute-done.1.rest_2_
  25.9 0.0 collective-permute-start.5
  25.9 0.5 %collective-permute-start.6 = (bf16[2,48,1024]{2,1,0:T(8,128)(2,1)S(1)}, bf16[2,48,1024]{2,1,0:T(8,128)(2,1)S(1)}, u32[]{:S(2)}, u32[]{:S(2)}) collective-permute-start(bf16[2,48,1024]{2,1,0:T(8,128)(2,1)S(1)} %collective-permute-done.2.rest_4_), channel_id=1, source_target_pairs={{0,1},{1,0},{2,3},{3,2},{4,5},{5,4},{6,7},{7,6},{8,9},{9,8},{10,11... | collective-permute-start | bytes 589832 | tf_op jit(solution)/shard_map/ppermute | solution.py:533
  26.4 1.3 %collective-permute-start.3 = (bf16[2,48,1024]{2,1,0:T(8,128)(2,1)S(1)}, bf16[2,48,1024]{2,1,0:T(8,128)(2,1)S(1)}, u32[]{:S(2)}, u32[]{:S(2)}) collective-permute-start(bf16[2,48,1024]{2,1,0:T(8,128)(2,1)S(1)} %collective-permute-done.2.rest_4_), channel_id=1, source_target_pairs={{0,2},{1,3},{2,0},{3,1},{4,6},{5,7},{6,4},{7,5},{8,10},{9,11},{10,... | collective-permute-start | bytes 589832 | tf_op jit(solution)/shard_map/ppermute | solution.py:538
  27.7 0.0 collective-permute-done.4.rest_1_
  27.7 0.0 collective-permute-done.5.rest_3_
  27.7 0.0 collective-permute-done.6.rest_5_
  27.7 0.0 copy-done.4
  27.7 6.2 %block_rows.2.rest_2_ = f32[12,2,24,2,1024]{4,3,2,1,0:T(2,128)} custom-call(s32[1,2]{1,0:T(1,128)S(1)} %bitcast.11, bf16[2,4,6,48,1024]{4,3,2,1,0:T(8,128)(2,1)S(1)} %prepare.1.turned_ref, bf16[1024,512]{1,0:T(8,128)(2,1)S(1)} %get-tuple-element.18.even_ref, bf16[1024,512]{1,0:T(8,128)(2,1)S(1)} %get-tuple-element.19.odd_ref, ...), custom_call_target="tpu_custom_call" | custom-call | flops 1811939328 | bytes 8388608 | tf_op jit(solution)/shard_map/block_rows/pallas_call | solution.py:503
  33.9 0.0 collective-permute-done.3.rest_0_
  33.9 0.2 collective-permute-start.7
  34.1 1.3 %collective-permute-done.7.rest_1_ = bf16[2,48,1024]{2,1,0:T(8,128)(2,1)S(1)} collective-permute-done((bf16[2,48,1024]{2,1,0:T(8,128)(2,1)S(1)}, bf16[2,48,1024]{2,1,0:T(8,128)(2,1)S(1)}, u32[]{:S(2)}, u32[]{:S(2)}) %collective-permute-start.7) | collective-permute-done | bytes 196640 | tf_op jit(solution)/shard_map/ppermute | solution.py:533
  35.5 2.6 %block_rows.3 = f32[12,2,24,2,1024]{4,3,2,1,0:T(2,128)} custom-call(s32[1,2]{1,0:T(1,128)S(1)} %bitcast.12, bf16[2,4,6,48,1024]{4,3,2,1,0:T(8,128)(2,1)S(1)} %prepare.1.turned_ref, bf16[1024,512]{1,0:T(8,128)(2,1)S(1)} %get-tuple-element.18.even_ref, bf16[1024,512]{1,0:T(8,128)(2,1)S(1)} %get-tuple-element.19.odd_ref, ...), custom_call_target="tpu_custom_call", output_to_operand_aliasing={{}: (6, {})} | custom-call | flops 603979776 | bytes 8388608 | tf_op jit(solution)/shard_map/block_rows/pallas_call | solution.py:503
Async XLA Ops:
  0.0 9.0 %copy-start.3 = (s32[4,2]{0,1:T(2,128)S(1)}, s32[4,2]{0,1:T(2,128)}, u32[]{:S(2)}) copy-start(s32[4,2]{0,1:T(2,128)} %param.14) | copy-start | bytes 100
  5.9 5.4 %copy-start = (f32[2,256,512]{2,1,0:T(8,128)S(1)}, f32[2,256,512]{2,1,0:T(8,128)}, u32[]{:S(2)}) copy-start(f32[2,256,512]{2,1,0:T(8,128)} %constant.19.clone.base_ref) | copy-start | bytes 3145732
  5.9 11.2 %collective-permute-start = (bf16[2,48,1024]{2,1,0:T(8,128)(2,1)}, bf16[2,48,1024]{2,1,0:T(8,128)(2,1)S(1)}, u32[]{:S(2)}, u32[]{:S(2)}) collective-permute-start(bf16[2,48,1024]{2,1,0:T(8,128)(2,1)} %spectra.1.sent_ref), channel_id=1, source_target_pairs={{28,0},{0,4},{4,8},{8,12},{12,16},{16,20},{20,24},{24,28},{29,1},{... | collective-permute-start | bytes 589832 | tf_op jit(solution)/shard_map/ppermute | solution.py:528
  9.0 1.0 %copy-start.1 = (bf16[2,48,1024]{2,1,0:T(8,128)(2,1)S(1)}, bf16[2,48,1024]{2,1,0:T(8,128)(2,1)}, u32[]{:S(2)}) copy-start(bf16[2,48,1024]{2,1,0:T(8,128)(2,1)} %spectra.1.sent_ref) | copy-start | bytes 589828
  10.0 1.3 %copy-start.2 = (f32[2,16,512]{2,1,0:T(8,128)S(1)}, f32[2,16,512]{2,1,0:T(8,128)}, u32[]{:S(2)}) copy-start(f32[2,16,512]{2,1,0:T(8,128)} %constant.20.clone.shift_ref) | copy-start | bytes 196612
  10.0 17.8 %copy-start.4 = (s32[2]{0:T(128)S(1)}, s32[2]{0:T(128)}, u32[]{:S(2)}) copy-start(s32[2]{0:T(128)} %param.16) | copy-start | bytes 28
  17.1 8.8 %collective-permute-start.2 = (bf16[2,48,1024]{2,1,0:T(8,128)(2,1)S(1)}, bf16[2,48,1024]{2,1,0:T(8,128)(2,1)S(1)}, u32[]{:S(2)}, u32[]{:S(2)}) collective-permute-start(bf16[2,48,1024]{2,1,0:T(8,128)(2,1)S(1)} %collective-permute-done.rest_0_), channel_id=1, source_target_pairs={{28,0},{0,4},{4,8},{8,12},{12,16},{16,20},{20,24},{24,28},{29,1},{... | collective-permute-start | bytes 589832 | tf_op jit(solution)/shard_map/ppermute | solution.py:528
  17.1 8.8 %collective-permute-start.1 = (bf16[2,48,1024]{2,1,0:T(8,128)(2,1)S(1)}, bf16[2,48,1024]{2,1,0:T(8,128)(2,1)S(1)}, u32[]{:S(2)}, u32[]{:S(2)}) collective-permute-start(bf16[2,48,1024]{2,1,0:T(8,128)(2,1)S(1)} %collective-permute-done.rest_0_), channel_id=1, source_target_pairs={{0,2},{1,3},{2,0},{3,1},{4,6},{5,7},{6,4},{7,5},{8,10},{9,11},{10,... | collective-permute-start | bytes 589832 | tf_op jit(solution)/shard_map/ppermute | solution.py:538
  18.6 9.1 %collective-permute-start.4 = (bf16[2,48,1024]{2,1,0:T(8,128)(2,1)S(1)}, bf16[2,48,1024]{2,1,0:T(8,128)(2,1)S(1)}, u32[]{:S(2)}, u32[]{:S(2)}) collective-permute-start(bf16[2,48,1024]{2,1,0:T(8,128)(2,1)S(1)} %collective-permute-done.rest_0_), channel_id=1, source_target_pairs={{0,1},{1,0},{2,3},{3,2},{4,5},{5,4},{6,7},{7,6},{8,9},{9,8},{10,11... | collective-permute-start | bytes 589832 | tf_op jit(solution)/shard_map/ppermute | solution.py:533
  25.9 1.8 %collective-permute-start.5 = (bf16[2,48,1024]{2,1,0:T(8,128)(2,1)S(1)}, bf16[2,48,1024]{2,1,0:T(8,128)(2,1)S(1)}, u32[]{:S(2)}, u32[]{:S(2)}) collective-permute-start(bf16[2,48,1024]{2,1,0:T(8,128)(2,1)S(1)} %collective-permute-done.1.rest_2_), channel_id=1, source_target_pairs={{0,1},{1,0},{2,3},{3,2},{4,5},{5,4},{6,7},{7,6},{8,9},{9,8},{10,11... | collective-permute-start | bytes 589832 | tf_op jit(solution)/shard_map/ppermute | solution.py:533
  25.9 1.8 %collective-permute-start.6 = (bf16[2,48,1024]{2,1,0:T(8,128)(2,1)S(1)}, bf16[2,48,1024]{2,1,0:T(8,128)(2,1)S(1)}, u32[]{:S(2)}, u32[]{:S(2)}) collective-permute-start(bf16[2,48,1024]{2,1,0:T(8,128)(2,1)S(1)} %collective-permute-done.2.rest_4_), channel_id=1, source_target_pairs={{0,1},{1,0},{2,3},{3,2},{4,5},{5,4},{6,7},{7,6},{8,9},{9,8},{10,11... | collective-permute-start | bytes 589832 | tf_op jit(solution)/shard_map/ppermute | solution.py:533
  26.4 7.5 %collective-permute-start.3 = (bf16[2,48,1024]{2,1,0:T(8,128)(2,1)S(1)}, bf16[2,48,1024]{2,1,0:T(8,128)(2,1)S(1)}, u32[]{:S(2)}, u32[]{:S(2)}) collective-permute-start(bf16[2,48,1024]{2,1,0:T(8,128)(2,1)S(1)} %collective-permute-done.2.rest_4_), channel_id=1, source_target_pairs={{0,2},{1,3},{2,0},{3,1},{4,6},{5,7},{6,4},{7,5},{8,10},{9,11},{10,... | collective-permute-start | bytes 589832 | tf_op jit(solution)/shard_map/ppermute | solution.py:538
  33.9 1.5 %collective-permute-start.7 = (bf16[2,48,1024]{2,1,0:T(8,128)(2,1)S(1)}, bf16[2,48,1024]{2,1,0:T(8,128)(2,1)S(1)}, u32[]{:S(2)}, u32[]{:S(2)}) collective-permute-start(bf16[2,48,1024]{2,1,0:T(8,128)(2,1)S(1)} %collective-permute-done.3.rest_0_), channel_id=1, source_target_pairs={{0,1},{1,0},{2,3},{3,2},{4,5},{5,4},{6,7},{7,6},{8,9},{9,8},{10,11... | collective-permute-start | bytes 589832 | tf_op jit(solution)/shard_map/ppermute | solution.py:533

commit v2 on v1

--- a/solution.py
+++ b/solution.py
@@ -416,16 +416,15 @@
             cross_im[at, lanes] = (im[0] + im[1]) + (im[2] + im[3])
 
 
-def mirrored(i, even, odd, value_ref):
-    _, peers, _ = value_ref.shape
+def mirrored(i, columns, even, odd, value_ref):
+    peers, width = even.shape
     backward = 127 - lax.broadcasted_iota(jnp.int32, (peers, 128), 1)
-    middle = LAGS // 256
-    for tile in range(HALF // 128):
-        lanes = slice(tile * 128, (tile + 1) * 128)
-        e, o = even[:, lanes], odd[:, lanes]
-        after, before = (middle + tile) * 128, (middle - 1 - tile) * 128
-        value_ref[i, :, after : after + 128] = e - o
-        value_ref[i, :, before : before + 128] = jnp.take_along_axis(e + o, backward, axis=1)
+    for tile in range(0, width, 128):
+        e, o = even[:, tile : tile + 128], odd[:, tile : tile + 128]
+        after = pl.multiple_of(HALF + columns + tile, 128)
+        before = pl.multiple_of(HALF - columns - tile - 128, 128)
+        value_ref[i, :, pl.ds(after, 128)] = e - o
+        value_ref[i, :, pl.ds(before, 128)] = jnp.take_along_axis(e + o, backward, axis=1)
 
 
 def started(i, value_ref, out_ref, block, distance, sems):
@@ -444,49 +443,36 @@
     rows = out_ref.shape[0]
     total = turned_ref.shape[2] * turned_ref.shape[3]
     peers = total // rows
-    bands = [slice(band * SLOT, (band + 1) * SLOT) for band in range(NBANDS)]
     copies = []
-
-    def cross(at, band):
-        crossed(
-            nw,
-            rows,
-            live_ref[:, units[at][0] : units[at][0] + 1].astype(f32),
-            bands[band],
-            turned_ref,
-            *sources[2 * at : 2 * at + 2],
-            cross_re.at[at],
-            cross_im.at[at],
-        )
-
-    def summed(at, lanes):
-        even = jnp.dot(cross_re[at, :, lanes], even_ref[lanes, :], preferred_element_type=f32)
-        odd = jnp.dot(cross_im[at, :, lanes], odd_ref[lanes, :], preferred_element_type=f32)
-        return even, odd
-
-    def finished(at, even, odd):
-        block, distance = units[at]
+    width = HALF // 2
+    for at, (block, distance) in enumerate(units):
+        live = live_ref[:, block : block + 1].astype(f32)
+
+        @pl.loop(0, NBANDS)
+        def cross(band):
+            crossed(
+                nw,
+                rows,
+                live,
+                pl.ds(pl.multiple_of(band * SLOT, SLOT), SLOT),
+                turned_ref,
+                *sources[2 * at : 2 * at + 2],
+                cross_re.at[at],
+                cross_im.at[at],
+            )
+
+        @pl.loop(0, HALF // width)
+        def lags(step):
+            columns = pl.multiple_of(step * width, width)
+            some = pl.ds(columns, width)
+            even = jnp.dot(cross_re[at], even_ref[:, some], preferred_element_type=f32)
+            odd = jnp.dot(cross_im[at], odd_ref[:, some], preferred_element_type=f32)
+            for i in range(rows):
+                span = slice(i * peers, (i + 1) * peers)
+                mirrored(i, columns, even[span], odd[span], values.at[at])
+
         for i in range(rows):
-            span = slice(i * peers, (i + 1) * peers)
-            mirrored(i, even[span], odd[span], values.at[at])
             copies.append(started(i, values.at[at], out_ref, block, distance, sems.at[at]))
-
-    if len(units) == 1:
-        half = NBANDS // 2
-        parts = []
-        for first in (0, half):
-            for band in range(first, first + half):
-                cross(0, band)
-            parts.append(summed(0, slice(first * SLOT, (first + half) * SLOT)))
-        (even, odd), (more_even, more_odd) = parts
-        finished(0, even + more_even, odd + more_odd)
-    else:
-        for at in range(len(units) + 1):
-            if at < len(units):
-                for band in range(NBANDS):
-                    cross(at, band)
-            if at:
-                finished(at - 1, *summed(at - 1, slice(0, KEPT)))
     for copy in copies:
         copy.wait()
 

time: 38.3 us -> 40.3 us (1.052)
  Pallas kernels: 17.7 us -> 19.7 us
    pallas_call x2, Pallas kernels: 8.84 us -> 10.9 us  [correlate(): pl.pallas_call(functools.partial(correlate_kernel, nw, units, bool(more))...]
  transfers between devices with their start and end apart: 8 -> 8, of which waited for: 3 -> 3; matrix products, arithmetic and copies ran while one was open for 0% -> 0% of each run, Pallas kernels for 24% -> 26%
where the time goes in v2:
time: 40.3 us; the launch traced here: 40.2 us
  Pallas kernels  19.7 us (49%)
  waiting for transfers between devices  12.8 us (32%)
  starting transfers between devices  6.59 us (16%)
  local copies, waits for them, and re-layouts  0.98 us (2%)
    ppermute x2, waiting for transfers between devices, next_group(): return lax.ppermute(block, axes, [((i - 1) % n, i) for i in range(n)])  11.5 us
    pallas_call x2, Pallas kernels, correlate(): pl.pallas_call(functools.partial(correlate_kernel, nw, units, bool(more))...  10.9 us
    pallas_call x1, Pallas kernels, spectra(): pl.pallas_call(spectra_kernel, out_shape=jax.ShapeDtypeStruct((2, nw * gr...  5.91 us
    ppermute x2, starting transfers between devices, next_group(): return lax.ppermute(block, axes, [((i - 1) % n, i) for i in range(n)])  3.08 us
    ppermute x2, starting transfers between devices, from_chip(): lax.ppermute(block, 'sta', [(i, (i + 2 * distance) % n) for i in range(n)])  2.81 us
    pallas_call x1, Pallas kernels, lag_tables(): pl.pallas_call(lag_kernel, out_shape=[table, table], in_specs=[smem, vmem...  1.63 us
    ppermute x4, waiting for transfers between devices, swapped_core(): return lax.ppermute(block, 'sta', [(i, i ^ 1) for i in range(n)])  1.33 us
    pallas_call x1, Pallas kernels, prepare(): pl.pallas_call(functools.partial(prepare_kernel, peers), out_shape=jax.Sh...  1.29 us
  transfers between devices with their start and end apart: 8, of which 3 were waited for; matrix products, arithmetic and copies ran while one was open for 0% of the time, Pallas kernels for 26%

profile of v2, /device:TPU:0, one launch (start us, length us, event | category | flops | bytes accessed | tf_op | source)
XLA Modules:
  0.0 40.2 jit_solution(14912592340174198338)
XLA Ops:
  0.0 0.0 copy-start.3
  0.0 5.9 %spectra.1.sent_ref = bf16[2,48,1024]{2,1,0:T(8,128)(2,1)} custom-call(bf16[12,4,16384]{2,1,0:T(4,128)(2,1)} %bitcast.13, f32[1,64]{1,0:T(1,128)} %bitcast.14, s32[2,4]{1,0:T(2,128)} %bitcast.8, s32[1,4]{1,0:T(1,128)} %bitcast.15, bf16[2,512,128]{2,1,0:T(8,128)(2,1)} %constant.14.clone.table_hbm, f32[2,16,256]{2,1,0:T(8,128)} %constant.15.clone.twiddle_hbm, ...), custom_call_target="tpu_custom_call" | custom-call | flops 3000000000 | bytes 5242880 | tf_op jit(solution)/shard_map/spectra/pallas_call | solution.py:290
  5.9 0.0 copy-start
  5.9 3.1 %collective-permute-start = (bf16[2,48,1024]{2,1,0:T(8,128)(2,1)}, bf16[2,48,1024]{2,1,0:T(8,128)(2,1)S(1)}, u32[]{:S(2)}, u32[]{:S(2)}) collective-permute-start(bf16[2,48,1024]{2,1,0:T(8,128)(2,1)} %spectra.1.sent_ref), channel_id=1, source_target_pairs={{28,0},{0,4},{4,8},{8,12},{12,16},{16,20},{20,24},{24,28},{29,1},{... | collective-permute-start | bytes 589832 | tf_op jit(solution)/shard_map/ppermute | solution.py:514
  9.0 0.0 copy-done.3
  9.0 0.0 copy-start.1
  9.0 1.0 %copy-done.1 = bf16[2,48,1024]{2,1,0:T(8,128)(2,1)S(1)} copy-done((bf16[2,48,1024]{2,1,0:T(8,128)(2,1)S(1)}, bf16[2,48,1024]{2,1,0:T(8,128)(2,1)}, u32[]{:S(2)}) %copy-start.1) | copy-done | bytes 196632
  10.0 0.0 copy-start.2
  10.0 0.0 copy-start.4
  10.0 1.3 %prepare.1.turned_ref = bf16[2,4,6,48,1024]{4,3,2,1,0:T(8,128)(2,1)S(1)} custom-call(s32[2,4]{1,0:T(2,128)S(1)} %bitcast.9, bf16[2,48,1024]{2,1,0:T(8,128)(2,1)S(1)} %copy-done.1), custom_call_target="tpu_custom_call" | custom-call | flops 10000000 | bytes 4194304 | tf_op jit(solution)/shard_map/prepare/pallas_call | solution.py:339
  11.3 0.0 copy-done
  11.3 0.0 copy-done.2
  11.3 1.6 %lag_tables.1 = (bf16[1024,512]{1,0:T(8,128)(2,1)S(1)}, bf16[1024,512]{1,0:T(8,128)(2,1)S(1)}) custom-call(s32[2,4]{1,0:T(2,128)S(1)} %bitcast.10, f32[2,256,512]{2,1,0:T(8,128)S(1)} %copy-done, f32[2,16,512]{2,1,0:T(8,128)S(1)} %copy-done.2), custom_call_target="tpu_custom_call" | custom-call | flops 10000000 | bytes 4194304 | tf_op jit(solution)/shard_map/lag_tables/pallas_call | solution.py:373
  12.9 4.2 %collective-permute-done.rest_0_ = bf16[2,48,1024]{2,1,0:T(8,128)(2,1)S(1)} collective-permute-done((bf16[2,48,1024]{2,1,0:T(8,128)(2,1)}, bf16[2,48,1024]{2,1,0:T(8,128)(2,1)S(1)}, u32[]{:S(2)}, u32[]{:S(2)}) %collective-permute-start) | collective-permute-done | bytes 196640 | tf_op jit(solution)/shard_map/ppermute | solution.py:514
  17.1 0.0 collective-permute-start.2
  17.1 1.5 %collective-permute-start.1 = (bf16[2,48,1024]{2,1,0:T(8,128)(2,1)S(1)}, bf16[2,48,1024]{2,1,0:T(8,128)(2,1)S(1)}, u32[]{:S(2)}, u32[]{:S(2)}) collective-permute-start(bf16[2,48,1024]{2,1,0:T(8,128)(2,1)S(1)} %collective-permute-done.rest_0_), channel_id=1, source_target_pairs={{0,2},{1,3},{2,0},{3,1},{4,6},{5,7},{6,4},{7,5},{8,10},{9,11},{10,... | collective-permute-start | bytes 589832 | tf_op jit(solution)/shard_map/ppermute | solution.py:524
  18.6 0.0 collective-permute-start.4
  18.6 7.3 %collective-permute-done.2.rest_4_ = bf16[2,48,1024]{2,1,0:T(8,128)(2,1)S(1)} collective-permute-done((bf16[2,48,1024]{2,1,0:T(8,128)(2,1)S(1)}, bf16[2,48,1024]{2,1,0:T(8,128)(2,1)S(1)}, u32[]{:S(2)}, u32[]{:S(2)}) %collective-permute-start.2) | collective-permute-done | bytes 196640 | tf_op jit(solution)/shard_map/ppermute | solution.py:514
  25.9 0.0 collective-permute-done.1.rest_2_
  25.9 0.0 collective-permute-start.5
  25.9 0.5 %collective-permute-start.6 = (bf16[2,48,1024]{2,1,0:T(8,128)(2,1)S(1)}, bf16[2,48,1024]{2,1,0:T(8,128)(2,1)S(1)}, u32[]{:S(2)}, u32[]{:S(2)}) collective-permute-start(bf16[2,48,1024]{2,1,0:T(8,128)(2,1)S(1)} %collective-permute-done.2.rest_4_), channel_id=1, source_target_pairs={{0,1},{1,0},{2,3},{3,2},{4,5},{5,4},{6,7},{7,6},{8,9},{9,8},{10,11... | collective-permute-start | bytes 589832 | tf_op jit(solution)/shard_map/ppermute | solution.py:519
  26.4 1.3 %collective-permute-start.3 = (bf16[2,48,1024]{2,1,0:T(8,128)(2,1)S(1)}, bf16[2,48,1024]{2,1,0:T(8,128)(2,1)S(1)}, u32[]{:S(2)}, u32[]{:S(2)}) collective-permute-start(bf16[2,48,1024]{2,1,0:T(8,128)(2,1)S(1)} %collective-permute-done.2.rest_4_), channel_id=1, source_target_pairs={{0,2},{1,3},{2,0},{3,1},{4,6},{5,7},{6,4},{7,5},{8,10},{9,11},{10,... | collective-permute-start | bytes 589832 | tf_op jit(solution)/shard_map/ppermute | solution.py:524
  27.7 0.0 collective-permute-done.4.rest_1_
  27.7 0.0 collective-permute-done.5.rest_3_
  27.7 0.0 collective-permute-done.6.rest_5_
  27.7 0.0 copy-done.4
  27.7 7.7 %block_rows.2.rest_2_ = f32[12,2,24,2,1024]{4,3,2,1,0:T(2,128)} custom-call(s32[1,2]{1,0:T(1,128)S(1)} %bitcast.11, bf16[2,4,6,48,1024]{4,3,2,1,0:T(8,128)(2,1)S(1)} %prepare.1.turned_ref, bf16[1024,512]{1,0:T(8,128)(2,1)S(1)} %get-tuple-element.18.even_ref, bf16[1024,512]{1,0:T(8,128)(2,1)S(1)} %get-tuple-element.19.odd_ref, ...), custom_call_target="tpu_custom_call" | custom-call | flops 1811939328 | bytes 8388608 | tf_op jit(solution)/shard_map/block_rows/pallas_call | solution.py:489
  35.5 0.0 collective-permute-done.3.rest_0_
  35.5 0.2 collective-permute-start.7
  35.7 1.3 %collective-permute-done.7.rest_1_ = bf16[2,48,1024]{2,1,0:T(8,128)(2,1)S(1)} collective-permute-done((bf16[2,48,1024]{2,1,0:T(8,128)(2,1)S(1)}, bf16[2,48,1024]{2,1,0:T(8,128)(2,1)S(1)}, u32[]{:S(2)}, u32[]{:S(2)}) %collective-permute-start.7) | collective-permute-done | bytes 196640 | tf_op jit(solution)/shard_map/ppermute | solution.py:519
  37.0 3.2 %block_rows.3 = f32[12,2,24,2,1024]{4,3,2,1,0:T(2,128)} custom-call(s32[1,2]{1,0:T(1,128)S(1)} %bitcast.12, bf16[2,4,6,48,1024]{4,3,2,1,0:T(8,128)(2,1)S(1)} %prepare.1.turned_ref, bf16[1024,512]{1,0:T(8,128)(2,1)S(1)} %get-tuple-element.18.even_ref, bf16[1024,512]{1,0:T(8,128)(2,1)S(1)} %get-tuple-element.19.odd_ref, ...), custom_call_target="tpu_custom_call", output_to_operand_aliasing={{}: (6, {})} | custom-call | flops 603979776 | bytes 8388608 | tf_op jit(solution)/shard_map/block_rows/pallas_call | solution.py:489
Async XLA Ops:
  0.0 9.0 %copy-start.3 = (s32[4,2]{0,1:T(2,128)S(1)}, s32[4,2]{0,1:T(2,128)}, u32[]{:S(2)}) copy-start(s32[4,2]{0,1:T(2,128)} %param.14) | copy-start | bytes 100
  5.9 5.4 %copy-start = (f32[2,256,512]{2,1,0:T(8,128)S(1)}, f32[2,256,512]{2,1,0:T(8,128)}, u32[]{:S(2)}) copy-start(f32[2,256,512]{2,1,0:T(8,128)} %constant.19.clone.base_ref) | copy-start | bytes 3145732
  5.9 11.2 %collective-permute-start = (bf16[2,48,1024]{2,1,0:T(8,128)(2,1)}, bf16[2,48,1024]{2,1,0:T(8,128)(2,1)S(1)}, u32[]{:S(2)}, u32[]{:S(2)}) collective-permute-start(bf16[2,48,1024]{2,1,0:T(8,128)(2,1)} %spectra.1.sent_ref), channel_id=1, source_target_pairs={{28,0},{0,4},{4,8},{8,12},{12,16},{16,20},{20,24},{24,28},{29,1},{... | collective-permute-start | bytes 589832 | tf_op jit(solution)/shard_map/ppermute | solution.py:514
  9.0 1.0 %copy-start.1 = (bf16[2,48,1024]{2,1,0:T(8,128)(2,1)S(1)}, bf16[2,48,1024]{2,1,0:T(8,128)(2,1)}, u32[]{:S(2)}) copy-start(bf16[2,48,1024]{2,1,0:T(8,128)(2,1)} %spectra.1.sent_ref) | copy-start | bytes 589828
  10.0 1.3 %copy-start.2 = (f32[2,16,512]{2,1,0:T(8,128)S(1)}, f32[2,16,512]{2,1,0:T(8,128)}, u32[]{:S(2)}) copy-start(f32[2,16,512]{2,1,0:T(8,128)} %constant.20.clone.shift_ref) | copy-start | bytes 196612
  10.0 17.8 %copy-start.4 = (s32[2]{0:T(128)S(1)}, s32[2]{0:T(128)}, u32[]{:S(2)}) copy-start(s32[2]{0:T(128)} %param.16) | copy-start | bytes 28
  17.1 8.8 %collective-permute-start.2 = (bf16[2,48,1024]{2,1,0:T(8,128)(2,1)S(1)}, bf16[2,48,1024]{2,1,0:T(8,128)(2,1)S(1)}, u32[]{:S(2)}, u32[]{:S(2)}) collective-permute-start(bf16[2,48,1024]{2,1,0:T(8,128)(2,1)S(1)} %collective-permute-done.rest_0_), channel_id=1, source_target_pairs={{28,0},{0,4},{4,8},{8,12},{12,16},{16,20},{20,24},{24,28},{29,1},{... | collective-permute-start | bytes 589832 | tf_op jit(solution)/shard_map/ppermute | solution.py:514
  17.1 8.8 %collective-permute-start.1 = (bf16[2,48,1024]{2,1,0:T(8,128)(2,1)S(1)}, bf16[2,48,1024]{2,1,0:T(8,128)(2,1)S(1)}, u32[]{:S(2)}, u32[]{:S(2)}) collective-permute-start(bf16[2,48,1024]{2,1,0:T(8,128)(2,1)S(1)} %collective-permute-done.rest_0_), channel_id=1, source_target_pairs={{0,2},{1,3},{2,0},{3,1},{4,6},{5,7},{6,4},{7,5},{8,10},{9,11},{10,... | collective-permute-start | bytes 589832 | tf_op jit(solution)/shard_map/ppermute | solution.py:524
  18.6 9.1 %collective-permute-start.4 = (bf16[2,48,1024]{2,1,0:T(8,128)(2,1)S(1)}, bf16[2,48,1024]{2,1,0:T(8,128)(2,1)S(1)}, u32[]{:S(2)}, u32[]{:S(2)}) collective-permute-start(bf16[2,48,1024]{2,1,0:T(8,128)(2,1)S(1)} %collective-permute-done.rest_0_), channel_id=1, source_target_pairs={{0,1},{1,0},{2,3},{3,2},{4,5},{5,4},{6,7},{7,6},{8,9},{9,8},{10,11... | collective-permute-start | bytes 589832 | tf_op jit(solution)/shard_map/ppermute | solution.py:519
  25.9 1.8 %collective-permute-start.5 = (bf16[2,48,1024]{2,1,0:T(8,128)(2,1)S(1)}, bf16[2,48,1024]{2,1,0:T(8,128)(2,1)S(1)}, u32[]{:S(2)}, u32[]{:S(2)}) collective-permute-start(bf16[2,48,1024]{2,1,0:T(8,128)(2,1)S(1)} %collective-permute-done.1.rest_2_), channel_id=1, source_target_pairs={{0,1},{1,0},{2,3},{3,2},{4,5},{5,4},{6,7},{7,6},{8,9},{9,8},{10,11... | collective-permute-start | bytes 589832 | tf_op jit(solution)/shard_map/ppermute | solution.py:519
  25.9 1.8 %collective-permute-start.6 = (bf16[2,48,1024]{2,1,0:T(8,128)(2,1)S(1)}, bf16[2,48,1024]{2,1,0:T(8,128)(2,1)S(1)}, u32[]{:S(2)}, u32[]{:S(2)}) collective-permute-start(bf16[2,48,1024]{2,1,0:T(8,128)(2,1)S(1)} %collective-permute-done.2.rest_4_), channel_id=1, source_target_pairs={{0,1},{1,0},{2,3},{3,2},{4,5},{5,4},{6,7},{7,6},{8,9},{9,8},{10,11... | collective-permute-start | bytes 589832 | tf_op jit(solution)/shard_map/ppermute | solution.py:519
  26.4 9.1 %collective-permute-start.3 = (bf16[2,48,1024]{2,1,0:T(8,128)(2,1)S(1)}, bf16[2,48,1024]{2,1,0:T(8,128)(2,1)S(1)}, u32[]{:S(2)}, u32[]{:S(2)}) collective-permute-start(bf16[2,48,1024]{2,1,0:T(8,128)(2,1)S(1)} %collective-permute-done.2.rest_4_), channel_id=1, source_target_pairs={{0,2},{1,3},{2,0},{3,1},{4,6},{5,7},{6,4},{7,5},{8,10},{9,11},{10,... | collective-permute-start | bytes 589832 | tf_op jit(solution)/shard_map/ppermute | solution.py:524
  35.5 1.5 %collective-permute-start.7 = (bf16[2,48,1024]{2,1,0:T(8,128)(2,1)S(1)}, bf16[2,48,1024]{2,1,0:T(8,128)(2,1)S(1)}, u32[]{:S(2)}, u32[]{:S(2)}) collective-permute-start(bf16[2,48,1024]{2,1,0:T(8,128)(2,1)S(1)} %collective-permute-done.3.rest_0_), channel_id=1, source_target_pairs={{0,1},{1,0},{2,3},{3,2},{4,5},{5,4},{6,7},{7,6},{8,9},{9,8},{10,11... | collective-permute-start | bytes 589832 | tf_op jit(solution)/shard_map/ppermute | solution.py:519

commit v3 on v1

--- a/solution.py
+++ b/solution.py
@@ -416,22 +416,23 @@
             cross_im[at, lanes] = (im[0] + im[1]) + (im[2] + im[3])
 
 
-def mirrored(i, even, odd, value_ref):
-    _, peers, _ = value_ref.shape
+def mirrored(i, columns, even, odd, value_ref):
+    peers, width = even.shape
     backward = 127 - lax.broadcasted_iota(jnp.int32, (peers, 128), 1)
-    middle = LAGS // 256
-    for tile in range(HALF // 128):
-        lanes = slice(tile * 128, (tile + 1) * 128)
-        e, o = even[:, lanes], odd[:, lanes]
-        after, before = (middle + tile) * 128, (middle - 1 - tile) * 128
+    for tile in range(0, width, 128):
+        e, o = even[:, tile : tile + 128], odd[:, tile : tile + 128]
+        after = HALF + columns + tile
+        before = HALF - columns - tile - 128
         value_ref[i, :, after : after + 128] = e - o
         value_ref[i, :, before : before + 128] = jnp.take_along_axis(e + o, backward, axis=1)
 
 
-def started(i, value_ref, out_ref, block, distance, sems):
+def started(lanes, value_ref, out_ref, block, distance, sem):
     _, chips, _, _, _ = out_ref.shape
     chip = lax.rem(lax.axis_index("sta") // 2 + chips - distance, chips)
-    copy = pltpu.make_async_copy(value_ref.at[i], out_ref.at[i, chip, :, block, :], sems.at[i])
+    copy = pltpu.make_async_copy(
+        value_ref.at[:, :, lanes], out_ref.at[:, chip, :, block, lanes], sem
+    )
     copy.start()
     return copy
 
@@ -459,34 +460,32 @@
             cross_im.at[at],
         )
 
-    def summed(at, lanes):
-        even = jnp.dot(cross_re[at, :, lanes], even_ref[lanes, :], preferred_element_type=f32)
-        odd = jnp.dot(cross_im[at, :, lanes], odd_ref[lanes, :], preferred_element_type=f32)
-        return even, odd
-
-    def finished(at, even, odd):
+    width = HALF // 2
+
+    def finished(at, step):
         block, distance = units[at]
+        columns = step * width
+        some = slice(columns, columns + width)
+        even = jnp.dot(cross_re[at], even_ref[:, some], preferred_element_type=f32)
+        odd = jnp.dot(cross_im[at], odd_ref[:, some], preferred_element_type=f32)
         for i in range(rows):
             span = slice(i * peers, (i + 1) * peers)
-            mirrored(i, even[span], odd[span], values.at[at])
-            copies.append(started(i, values.at[at], out_ref, block, distance, sems.at[at]))
-
-    if len(units) == 1:
-        half = NBANDS // 2
-        parts = []
-        for first in (0, half):
-            for band in range(first, first + half):
-                cross(0, band)
-            parts.append(summed(0, slice(first * SLOT, (first + half) * SLOT)))
-        (even, odd), (more_even, more_odd) = parts
-        finished(0, even + more_even, odd + more_odd)
-    else:
-        for at in range(len(units) + 1):
+            mirrored(i, columns, even[span], odd[span], values.at[at])
+        if step == 0:
+            made = [pl.ds(HALF - width, 2 * width)]
+        else:
+            made = [pl.ds(0, HALF - width), pl.ds(HALF + width, HALF - width)]
+        for n, lanes in enumerate(made):
+            sem = sems.at[at, step + n]
+            copies.append(started(lanes, values.at[at], out_ref, block, distance, sem))
+
+    for at in range(len(units) + 1):
+        for step in range(2):
             if at < len(units):
-                for band in range(NBANDS):
+                for band in range(step * NBANDS // 2, (step + 1) * NBANDS // 2):
                     cross(at, band)
             if at:
-                finished(at - 1, *summed(at - 1, slice(0, KEPT)))
+                finished(at - 1, step)
     for copy in copies:
         copy.wait()
 
@@ -509,7 +508,7 @@
             cross,
             cross,
             pltpu.VMEM((n, rows, peers, LAGS), f32),
-            pltpu.SemaphoreType.DMA((n, rows)),
+            pltpu.SemaphoreType.DMA((n, 3)),
         ],
         input_output_aliases={len(operands): 0} if more else {},
         compiler_params=pltpu.CompilerParams(vmem_limit_bytes=(24 if more else 32) * 2**20),

time: 38.3 us -> 38.5 us (level)
  transfers between devices with their start and end apart: 8 -> 8, of which waited for: 3 -> 3; matrix products, arithmetic and copies ran while one was open for 0% -> 0% of each run, Pallas kernels for 24% -> 25%
where the time goes in v3:
time: 38.5 us; the launch traced here: 38.3 us
  Pallas kernels  17.9 us (46%)
  waiting for transfers between devices  12.8 us (33%)
  starting transfers between devices  6.57 us (17%)
  local copies, waits for them, and re-layouts  0.98 us (3%)
    ppermute x2, waiting for transfers between devices, next_group(): return lax.ppermute(block, axes, [((i - 1) % n, i) for i in range(n)])  11.5 us
    pallas_call x2, Pallas kernels, correlate(): pl.pallas_call(functools.partial(correlate_kernel, nw, units, bool(more))...  9.06 us
    pallas_call x1, Pallas kernels, spectra(): pl.pallas_call(spectra_kernel, out_shape=jax.ShapeDtypeStruct((2, nw * gr...  5.91 us
    ppermute x2, starting transfers between devices, next_group(): return lax.ppermute(block, axes, [((i - 1) % n, i) for i in range(n)])  3.08 us
    ppermute x2, starting transfers between devices, from_chip(): lax.ppermute(block, 'sta', [(i, (i + 2 * distance) % n) for i in range(n)])  2.81 us
    pallas_call x1, Pallas kernels, lag_tables(): pl.pallas_call(lag_kernel, out_shape=[table, table], in_specs=[smem, vmem...  1.63 us
    ppermute x4, waiting for transfers between devices, swapped_core(): return lax.ppermute(block, 'sta', [(i, i ^ 1) for i in range(n)])  1.34 us
    pallas_call x1, Pallas kernels, prepare(): pl.pallas_call(functools.partial(prepare_kernel, peers), out_shape=jax.Sh...  1.29 us
  transfers between devices with their start and end apart: 8, of which 3 were waited for; matrix products, arithmetic and copies ran while one was open for 0% of the time, Pallas kernels for 25%

profile of v3, /device:TPU:0, one launch (start us, length us, event | category | flops | bytes accessed | tf_op | source)
XLA Modules:
  0.0 38.3 jit_solution(1412628131824003382)
XLA Ops:
  0.0 0.0 copy-start.3
  0.0 5.9 %spectra.1.sent_ref = bf16[2,48,1024]{2,1,0:T(8,128)(2,1)} custom-call(bf16[12,4,16384]{2,1,0:T(4,128)(2,1)} %bitcast.13, f32[1,64]{1,0:T(1,128)} %bitcast.14, s32[2,4]{1,0:T(2,128)} %bitcast.8, s32[1,4]{1,0:T(1,128)} %bitcast.15, bf16[2,512,128]{2,1,0:T(8,128)(2,1)} %constant.14.clone.table_hbm, f32[2,16,256]{2,1,0:T(8,128)} %constant.15.clone.twiddle_hbm, ...), custom_call_target="tpu_custom_call" | custom-call | flops 3000000000 | bytes 5242880 | tf_op jit(solution)/shard_map/spectra/pallas_call | solution.py:290
  5.9 0.0 copy-start
  5.9 3.1 %collective-permute-start = (bf16[2,48,1024]{2,1,0:T(8,128)(2,1)}, bf16[2,48,1024]{2,1,0:T(8,128)(2,1)S(1)}, u32[]{:S(2)}, u32[]{:S(2)}) collective-permute-start(bf16[2,48,1024]{2,1,0:T(8,128)(2,1)} %spectra.1.sent_ref), channel_id=1, source_target_pairs={{28,0},{0,4},{4,8},{8,12},{12,16},{16,20},{20,24},{24,28},{29,1},{... | collective-permute-start | bytes 589832 | tf_op jit(solution)/shard_map/ppermute | solution.py:527
  9.0 0.0 copy-done.3
  9.0 0.0 copy-start.1
  9.0 1.0 %copy-done.1 = bf16[2,48,1024]{2,1,0:T(8,128)(2,1)S(1)} copy-done((bf16[2,48,1024]{2,1,0:T(8,128)(2,1)S(1)}, bf16[2,48,1024]{2,1,0:T(8,128)(2,1)}, u32[]{:S(2)}) %copy-start.1) | copy-done | bytes 196632
  10.0 0.0 copy-start.2
  10.0 0.0 copy-start.4
  10.0 1.3 %prepare.1.turned_ref = bf16[2,4,6,48,1024]{4,3,2,1,0:T(8,128)(2,1)S(1)} custom-call(s32[2,4]{1,0:T(2,128)S(1)} %bitcast.9, bf16[2,48,1024]{2,1,0:T(8,128)(2,1)S(1)} %copy-done.1), custom_call_target="tpu_custom_call" | custom-call | flops 10000000 | bytes 4194304 | tf_op jit(solution)/shard_map/prepare/pallas_call | solution.py:339
  11.3 0.0 copy-done
  11.3 0.0 copy-done.2
  11.3 1.6 %lag_tables.1 = (bf16[1024,512]{1,0:T(8,128)(2,1)S(1)}, bf16[1024,512]{1,0:T(8,128)(2,1)S(1)}) custom-call(s32[2,4]{1,0:T(2,128)S(1)} %bitcast.10, f32[2,256,512]{2,1,0:T(8,128)S(1)} %copy-done, f32[2,16,512]{2,1,0:T(8,128)S(1)} %copy-done.2), custom_call_target="tpu_custom_call" | custom-call | flops 10000000 | bytes 4194304 | tf_op jit(solution)/shard_map/lag_tables/pallas_call | solution.py:373
  12.9 4.2 %collective-permute-done.rest_0_ = bf16[2,48,1024]{2,1,0:T(8,128)(2,1)S(1)} collective-permute-done((bf16[2,48,1024]{2,1,0:T(8,128)(2,1)}, bf16[2,48,1024]{2,1,0:T(8,128)(2,1)S(1)}, u32[]{:S(2)}, u32[]{:S(2)}) %collective-permute-start) | collective-permute-done | bytes 196640 | tf_op jit(solution)/shard_map/ppermute | solution.py:527
  17.1 0.0 collective-permute-start.2
  17.1 1.5 %collective-permute-start.1 = (bf16[2,48,1024]{2,1,0:T(8,128)(2,1)S(1)}, bf16[2,48,1024]{2,1,0:T(8,128)(2,1)S(1)}, u32[]{:S(2)}, u32[]{:S(2)}) collective-permute-start(bf16[2,48,1024]{2,1,0:T(8,128)(2,1)S(1)} %collective-permute-done.rest_0_), channel_id=1, source_target_pairs={{0,2},{1,3},{2,0},{3,1},{4,6},{5,7},{6,4},{7,5},{8,10},{9,11},{10,... | collective-permute-start | bytes 589832 | tf_op jit(solution)/shard_map/ppermute | solution.py:537
  18.6 0.0 collective-permute-start.4
  18.6 7.3 %collective-permute-done.2.rest_4_ = bf16[2,48,1024]{2,1,0:T(8,128)(2,1)S(1)} collective-permute-done((bf16[2,48,1024]{2,1,0:T(8,128)(2,1)S(1)}, bf16[2,48,1024]{2,1,0:T(8,128)(2,1)S(1)}, u32[]{:S(2)}, u32[]{:S(2)}) %collective-permute-start.2) | collective-permute-done | bytes 196640 | tf_op jit(solution)/shard_map/ppermute | solution.py:527
  25.9 0.0 collective-permute-done.1.rest_2_
  25.9 0.0 collective-permute-start.5
  25.9 0.5 %collective-permute-start.6 = (bf16[2,48,1024]{2,1,0:T(8,128)(2,1)S(1)}, bf16[2,48,1024]{2,1,0:T(8,128)(2,1)S(1)}, u32[]{:S(2)}, u32[]{:S(2)}) collective-permute-start(bf16[2,48,1024]{2,1,0:T(8,128)(2,1)S(1)} %collective-permute-done.2.rest_4_), channel_id=1, source_target_pairs={{0,1},{1,0},{2,3},{3,2},{4,5},{5,4},{6,7},{7,6},{8,9},{9,8},{10,11... | collective-permute-start | bytes 589832 | tf_op jit(solution)/shard_map/ppermute | solution.py:532
  26.4 1.3 %collective-permute-start.3 = (bf16[2,48,1024]{2,1,0:T(8,128)(2,1)S(1)}, bf16[2,48,1024]{2,1,0:T(8,128)(2,1)S(1)}, u32[]{:S(2)}, u32[]{:S(2)}) collective-permute-start(bf16[2,48,1024]{2,1,0:T(8,128)(2,1)S(1)} %collective-permute-done.2.rest_4_), channel_id=1, source_target_pairs={{0,2},{1,3},{2,0},{3,1},{4,6},{5,7},{6,4},{7,5},{8,10},{9,11},{10,... | collective-permute-start | bytes 589832 | tf_op jit(solution)/shard_map/ppermute | solution.py:537
  27.7 0.0 collective-permute-done.4.rest_1_
  27.7 0.0 collective-permute-done.5.rest_3_
  27.7 0.0 collective-permute-done.6.rest_5_
  27.7 0.0 copy-done.4
  27.7 6.7 %block_rows.2.rest_2_ = f32[12,2,24,2,1024]{4,3,2,1,0:T(2,128)} custom-call(s32[1,2]{1,0:T(1,128)S(1)} %bitcast.11, bf16[2,4,6,48,1024]{4,3,2,1,0:T(8,128)(2,1)S(1)} %prepare.1.turned_ref, bf16[1024,512]{1,0:T(8,128)(2,1)S(1)} %get-tuple-element.18.even_ref, bf16[1024,512]{1,0:T(8,128)(2,1)S(1)} %get-tuple-element.19.odd_ref, ...), custom_call_target="tpu_custom_call" | custom-call | flops 1811939328 | bytes 8388608 | tf_op jit(solution)/shard_map/block_rows/pallas_call | solution.py:502
  34.4 0.0 collective-permute-done.3.rest_0_
  34.4 0.2 collective-permute-start.7
  34.6 1.3 %collective-permute-done.7.rest_1_ = bf16[2,48,1024]{2,1,0:T(8,128)(2,1)S(1)} collective-permute-done((bf16[2,48,1024]{2,1,0:T(8,128)(2,1)S(1)}, bf16[2,48,1024]{2,1,0:T(8,128)(2,1)S(1)}, u32[]{:S(2)}, u32[]{:S(2)}) %collective-permute-start.7) | collective-permute-done | bytes 196640 | tf_op jit(solution)/shard_map/ppermute | solution.py:532
  35.9 2.4 %block_rows.3 = f32[12,2,24,2,1024]{4,3,2,1,0:T(2,128)} custom-call(s32[1,2]{1,0:T(1,128)S(1)} %bitcast.12, bf16[2,4,6,48,1024]{4,3,2,1,0:T(8,128)(2,1)S(1)} %prepare.1.turned_ref, bf16[1024,512]{1,0:T(8,128)(2,1)S(1)} %get-tuple-element.18.even_ref, bf16[1024,512]{1,0:T(8,128)(2,1)S(1)} %get-tuple-element.19.odd_ref, ...), custom_call_target="tpu_custom_call", output_to_operand_aliasing={{}: (6, {})} | custom-call | flops 603979776 | bytes 8388608 | tf_op jit(solution)/shard_map/block_rows/pallas_call | solution.py:502
Async XLA Ops:
  0.0 9.0 %copy-start.3 = (s32[4,2]{0,1:T(2,128)S(1)}, s32[4,2]{0,1:T(2,128)}, u32[]{:S(2)}) copy-start(s32[4,2]{0,1:T(2,128)} %param.14) | copy-start | bytes 100
  5.9 5.4 %copy-start = (f32[2,256,512]{2,1,0:T(8,128)S(1)}, f32[2,256,512]{2,1,0:T(8,128)}, u32[]{:S(2)}) copy-start(f32[2,256,512]{2,1,0:T(8,128)} %constant.19.clone.base_ref) | copy-start | bytes 3145732
  5.9 11.2 %collective-permute-start = (bf16[2,48,1024]{2,1,0:T(8,128)(2,1)}, bf16[2,48,1024]{2,1,0:T(8,128)(2,1)S(1)}, u32[]{:S(2)}, u32[]{:S(2)}) collective-permute-start(bf16[2,48,1024]{2,1,0:T(8,128)(2,1)} %spectra.1.sent_ref), channel_id=1, source_target_pairs={{28,0},{0,4},{4,8},{8,12},{12,16},{16,20},{20,24},{24,28},{29,1},{... | collective-permute-start | bytes 589832 | tf_op jit(solution)/shard_map/ppermute | solution.py:527
  9.0 1.0 %copy-start.1 = (bf16[2,48,1024]{2,1,0:T(8,128)(2,1)S(1)}, bf16[2,48,1024]{2,1,0:T(8,128)(2,1)}, u32[]{:S(2)}) copy-start(bf16[2,48,1024]{2,1,0:T(8,128)(2,1)} %spectra.1.sent_ref) | copy-start | bytes 589828
  10.0 1.3 %copy-start.2 = (f32[2,16,512]{2,1,0:T(8,128)S(1)}, f32[2,16,512]{2,1,0:T(8,128)}, u32[]{:S(2)}) copy-start(f32[2,16,512]{2,1,0:T(8,128)} %constant.20.clone.shift_ref) | copy-start | bytes 196612
  10.0 17.8 %copy-start.4 = (s32[2]{0:T(128)S(1)}, s32[2]{0:T(128)}, u32[]{:S(2)}) copy-start(s32[2]{0:T(128)} %param.16) | copy-start | bytes 28
  17.1 8.8 %collective-permute-start.2 = (bf16[2,48,1024]{2,1,0:T(8,128)(2,1)S(1)}, bf16[2,48,1024]{2,1,0:T(8,128)(2,1)S(1)}, u32[]{:S(2)}, u32[]{:S(2)}) collective-permute-start(bf16[2,48,1024]{2,1,0:T(8,128)(2,1)S(1)} %collective-permute-done.rest_0_), channel_id=1, source_target_pairs={{28,0},{0,4},{4,8},{8,12},{12,16},{16,20},{20,24},{24,28},{29,1},{... | collective-permute-start | bytes 589832 | tf_op jit(solution)/shard_map/ppermute | solution.py:527
  17.1 8.8 %collective-permute-start.1 = (bf16[2,48,1024]{2,1,0:T(8,128)(2,1)S(1)}, bf16[2,48,1024]{2,1,0:T(8,128)(2,1)S(1)}, u32[]{:S(2)}, u32[]{:S(2)}) collective-permute-start(bf16[2,48,1024]{2,1,0:T(8,128)(2,1)S(1)} %collective-permute-done.rest_0_), channel_id=1, source_target_pairs={{0,2},{1,3},{2,0},{3,1},{4,6},{5,7},{6,4},{7,5},{8,10},{9,11},{10,... | collective-permute-start | bytes 589832 | tf_op jit(solution)/shard_map/ppermute | solution.py:537
  18.6 9.1 %collective-permute-start.4 = (bf16[2,48,1024]{2,1,0:T(8,128)(2,1)S(1)}, bf16[2,48,1024]{2,1,0:T(8,128)(2,1)S(1)}, u32[]{:S(2)}, u32[]{:S(2)}) collective-permute-start(bf16[2,48,1024]{2,1,0:T(8,128)(2,1)S(1)} %collective-permute-done.rest_0_), channel_id=1, source_target_pairs={{0,1},{1,0},{2,3},{3,2},{4,5},{5,4},{6,7},{7,6},{8,9},{9,8},{10,11... | collective-permute-start | bytes 589832 | tf_op jit(solution)/shard_map/ppermute | solution.py:532
  25.9 1.8 %collective-permute-start.5 = (bf16[2,48,1024]{2,1,0:T(8,128)(2,1)S(1)}, bf16[2,48,1024]{2,1,0:T(8,128)(2,1)S(1)}, u32[]{:S(2)}, u32[]{:S(2)}) collective-permute-start(bf16[2,48,1024]{2,1,0:T(8,128)(2,1)S(1)} %collective-permute-done.1.rest_2_), channel_id=1, source_target_pairs={{0,1},{1,0},{2,3},{3,2},{4,5},{5,4},{6,7},{7,6},{8,9},{9,8},{10,11... | collective-permute-start | bytes 589832 | tf_op jit(solution)/shard_map/ppermute | solution.py:532
  25.9 1.8 %collective-permute-start.6 = (bf16[2,48,1024]{2,1,0:T(8,128)(2,1)S(1)}, bf16[2,48,1024]{2,1,0:T(8,128)(2,1)S(1)}, u32[]{:S(2)}, u32[]{:S(2)}) collective-permute-start(bf16[2,48,1024]{2,1,0:T(8,128)(2,1)S(1)} %collective-permute-done.2.rest_4_), channel_id=1, source_target_pairs={{0,1},{1,0},{2,3},{3,2},{4,5},{5,4},{6,7},{7,6},{8,9},{9,8},{10,11... | collective-permute-start | bytes 589832 | tf_op jit(solution)/shard_map/ppermute | solution.py:532
  26.4 8.0 %collective-permute-start.3 = (bf16[2,48,1024]{2,1,0:T(8,128)(2,1)S(1)}, bf16[2,48,1024]{2,1,0:T(8,128)(2,1)S(1)}, u32[]{:S(2)}, u32[]{:S(2)}) collective-permute-start(bf16[2,48,1024]{2,1,0:T(8,128)(2,1)S(1)} %collective-permute-done.2.rest_4_), channel_id=1, source_target_pairs={{0,2},{1,3},{2,0},{3,1},{4,6},{5,7},{6,4},{7,5},{8,10},{9,11},{10,... | collective-permute-start | bytes 589832 | tf_op jit(solution)/shard_map/ppermute | solution.py:537
  34.4 1.5 %collective-permute-start.7 = (bf16[2,48,1024]{2,1,0:T(8,128)(2,1)S(1)}, bf16[2,48,1024]{2,1,0:T(8,128)(2,1)S(1)}, u32[]{:S(2)}, u32[]{:S(2)}) collective-permute-start(bf16[2,48,1024]{2,1,0:T(8,128)(2,1)S(1)} %collective-permute-done.3.rest_0_), channel_id=1, source_target_pairs={{0,1},{1,0},{2,3},{3,2},{4,5},{5,4},{6,7},{7,6},{8,9},{9,8},{10,11... | collective-permute-start | bytes 589832 | tf_op jit(solution)/shard_map/ppermute | solution.py:532

commit v4 on v3

--- a/solution.py
+++ b/solution.py
@@ -27,7 +27,7 @@
 SPAN = DEC * FRAME
 LEAD = 256
 WINDOW = SPAN + LEAD
-PIECES = 4
+PIECES = 2
 BLOCKS_IN = NT // FRAME
 KEPT = NBANDS * SLOT
 EPS = 1e-06
@@ -63,13 +63,11 @@
     h = np.arange(RADIX)
     turn = 2.0 * np.pi * (h[:, None] * inner[None, :]) / NT
     twiddle = np.stack([np.cos(turn), -np.sin(turn)]).astype(np.float32)
-    place = np.zeros((TAPS, WINDOW), np.float32)
-    place[np.arange(TAPS), LEAD - np.arange(TAPS)] = 1.0
     fold = np.zeros((RADIX, BIG, SLOT), np.float32)
     for step in range(RADIX):
         fold[step, np.arange(BIG), FOLD * step + np.arange(BIG) % FOLD] = 1.0
     fold = by_tile(fold.reshape(BINS, SLOT).astype(bf16))
-    return by_tile(table.astype(np.float32).astype(bf16)), twiddle, by_tile(place.astype(bf16)), fold
+    return by_tile(table.astype(np.float32).astype(bf16)), twiddle, fold
 
 
 def lag_constants():
@@ -122,7 +120,6 @@
     live_hbm,
     table_hbm,
     twiddle_hbm,
-    place_hbm,
     fold_hbm,
     order_hbm,
     sent_ref,
@@ -132,7 +129,6 @@
     live_ref,
     table_ref,
     twiddle_ref,
-    place_ref,
     fold_ref,
     order_ref,
     turned,
@@ -141,7 +137,7 @@
 ):
     ch = x_ref.shape[0] * x_ref.shape[1]
     piece = RAW // PIECES
-    pairs = [(taps_hbm, taps_ref), (place_hbm, place_ref)]
+    pairs = [(taps_hbm, taps_ref)]
     for i in range(PIECES):
         lanes = slice(i * piece, (i + 1) * piece)
         pairs.append((x_hbm.at[:, :, lanes], x_ref.at[:, :, lanes]))
@@ -156,23 +152,26 @@
     copies = [pltpu.make_async_copy(a, b, sems.at[i]) for i, (a, b) in enumerate(pairs)]
     for copy in copies:
         copy.start()
+    tap = lax.broadcasted_iota(jnp.int32, (TAPS, WINDOW), 0)
+    place = (lax.broadcasted_iota(jnp.int32, (TAPS, WINDOW), 1) == LEAD - tap).astype(bf16)
     copies[0].wait()
     taps = taps_ref[...]
-    copies[1].wait()
     taps_high = taps.astype(bf16)
     taps_low = (taps - taps_high.astype(f32)).astype(bf16)
 
-    def toeplitz(part):
-        row = jnp.dot(part, joined(place_ref), preferred_element_type=f32)
+    parts = jnp.concatenate([taps_high, taps_low], axis=0)
+    placed = jnp.dot(parts, place, preferred_element_type=f32)
+
+    def toeplitz(row):
         return pltpu.roll(
             jnp.broadcast_to(row, (FRAME, WINDOW)), 0, 1, stride=DEC, stride_axis=0
         ).astype(bf16)
 
-    weights = jnp.concatenate([toeplitz(taps_high), toeplitz(taps_low)], axis=0)
+    weights = jnp.concatenate([toeplitz(placed[:1]), toeplitz(placed[1:])], axis=0)
     decimated = []
     tail = jnp.zeros((ch, LEAD), bf16)
     for i in range(PIECES):
-        copies[2 + i].wait()
+        copies[1 + i].wait()
         x = x_ref[:, :, i * piece : (i + 1) * piece].reshape(ch, piece)
         x = jnp.concatenate([tail, x], axis=1)
         tail = x[:, piece:]
@@ -185,7 +184,7 @@
         )
         decimated.append((both[:, :FRAME] + both[:, FRAME:]).astype(bf16).astype(f32))
     each = BLOCKS_IN // PIECES
-    copies[2 + PIECES].wait()
+    copies[1 + PIECES].wait()
     for at in range(0, ch, 16):
         d = []
         for b in range(RADIX):
@@ -207,7 +206,7 @@
                 where = slice(k * INNER, (k + 1) * INNER)
                 turned[h * ch + at : h * ch + at + 16, where] = u.astype(bf16)
 
-    for copy in copies[3 + PIECES :]:
+    for copy in copies[2 + PIECES :]:
         copy.wait()
     spectrum = jnp.dot(turned[...], joined(table_ref), preferred_element_type=f32)
 
@@ -427,26 +426,34 @@
         value_ref[i, :, before : before + 128] = jnp.take_along_axis(e + o, backward, axis=1)
 
 
-def started(lanes, value_ref, out_ref, block, distance, sem):
+def started(row, rows, lag, lags, value_ref, out_ref, block, distance, sem):
     _, chips, _, _, _ = out_ref.shape
     chip = lax.rem(lax.axis_index("sta") // 2 + chips - distance, chips)
+    mine, lanes = pl.ds(row, rows), pl.ds(lag, lags)
     copy = pltpu.make_async_copy(
-        value_ref.at[:, :, lanes], out_ref.at[:, chip, :, block, lanes], sem
+        value_ref.at[mine, :, lanes], out_ref.at[mine, chip, :, block, lanes], sem
     )
     copy.start()
     return copy
 
 
-def correlate_kernel(nw, units, aliased, live_ref, turned_ref, even_ref, odd_ref, *rest):
+def correlate_kernel(nw, units, written_by, live_ref, turned_ref, even_ref, odd_ref, *rest):
     sources, rest = rest[: 2 * len(units)], rest[2 * len(units) :]
-    if aliased:
-        rest = rest[1:]
-    out_ref, cross_re, cross_im, values, sems = rest
-    rows = out_ref.shape[0]
+    keeps, aliased, keeps_in = written_by
+    if keeps:
+        values, cross_re, cross_im = rest
+        values = [values]
+    else:
+        kept_ref = rest[1] if keeps_in else None
+        out_ref, cross_re, cross_im, values, sems = rest[aliased + keeps_in :]
+        values = [values.at[at] for at in range(len(units))]
+    rows = values[0].shape[0]
     total = turned_ref.shape[2] * turned_ref.shape[3]
     peers = total // rows
+    copies = []
+    if keeps_in:
+        copies.append(started(0, rows, 0, LAGS, kept_ref, out_ref, 1, 0, sems.at[len(units), 0]))
     bands = [slice(band * SLOT, (band + 1) * SLOT) for band in range(NBANDS)]
-    copies = []
 
     def cross(at, band):
         crossed(
@@ -462,35 +469,44 @@
 
     width = HALF // 2
 
-    def finished(at, step):
+    def finished(at, columns, width):
         block, distance = units[at]
-        columns = step * width
         some = slice(columns, columns + width)
         even = jnp.dot(cross_re[at], even_ref[:, some], preferred_element_type=f32)
         odd = jnp.dot(cross_im[at], odd_ref[:, some], preferred_element_type=f32)
+        whole = width == HALF
         for i in range(rows):
             span = slice(i * peers, (i + 1) * peers)
-            mirrored(i, columns, even[span], odd[span], values.at[at])
-        if step == 0:
-            made = [pl.ds(HALF - width, 2 * width)]
+            mirrored(i, columns, even[span], odd[span], values[at])
+            if whole:
+                copies.append(started(i, 1, 0, LAGS, values[at], out_ref, block, distance, sems.at[at, i]))
+        if whole or keeps:
+            return
+        if columns == 0:
+            made = [(HALF - width, 2 * width)]
         else:
-            made = [pl.ds(0, HALF - width), pl.ds(HALF + width, HALF - width)]
-        for n, lanes in enumerate(made):
-            sem = sems.at[at, step + n]
-            copies.append(started(lanes, values.at[at], out_ref, block, distance, sem))
-
-    for at in range(len(units) + 1):
+            made = [(0, HALF - columns), (HALF + columns, HALF - columns)]
+        for n, (first, count) in enumerate(made):
+            sem = sems.at[at, columns // width + n]
+            copies.append(started(0, rows, first, count, values[at], out_ref, block, distance, sem))
+
+    if len(units) == 1:
+        for band in range(NBANDS):
+            cross(0, band)
         for step in range(2):
+            finished(0, step * width, width)
+    else:
+        for at in range(len(units) + 1):
             if at < len(units):
-                for band in range(step * NBANDS // 2, (step + 1) * NBANDS // 2):
+                for band in range(NBANDS):
                     cross(at, band)
             if at:
-                finished(at - 1, step)
+                finished(at - 1, 0, HALF)
     for copy in copies:
         copy.wait()
 
 
-def correlate(block_live, turned, tables, rows, chips, units, sources, more=()):
+def correlate(block_live, turned, tables, rows, chips, units, sources, out=(), kept=(), keeps=False):
     _, nw, groups, group_rows, _ = turned.shape
     total = groups * group_rows
     peers = 2 * rows
@@ -499,26 +515,29 @@
     output = pl.BlockSpec(memory_space=pl.ANY)
     operands = [block_live, turned, *tables, *sources]
     cross = pltpu.VMEM((n, total, KEPT), bf16)
+    value = (rows, peers, LAGS)
+    scratch = [cross, cross]
+    if not keeps:
+        scratch += [
+            pltpu.VMEM((n,) + value, f32),
+            pltpu.SemaphoreType.DMA((n + 1, max(rows, 3))),
+        ]
+    shape = value if keeps else (rows, chips, peers, OFFS, LAGS)
     return pl.pallas_call(
-        functools.partial(correlate_kernel, nw, units, bool(more)),
-        out_shape=jax.ShapeDtypeStruct((rows, chips, peers, OFFS, LAGS), f32),
-        in_specs=[vmem] * len(operands) + [output] * len(more),
-        out_specs=output,
-        scratch_shapes=[
-            cross,
-            cross,
-            pltpu.VMEM((n, rows, peers, LAGS), f32),
-            pltpu.SemaphoreType.DMA((n, 3)),
-        ],
-        input_output_aliases={len(operands): 0} if more else {},
-        compiler_params=pltpu.CompilerParams(vmem_limit_bytes=(24 if more else 32) * 2**20),
+        functools.partial(correlate_kernel, nw, units, (keeps, len(out), len(kept))),
+        out_shape=jax.ShapeDtypeStruct(shape, f32),
+        in_specs=[vmem] * len(operands) + [output] * len(out) + [vmem] * len(kept),
+        out_specs=vmem if keeps else output,
+        scratch_shapes=scratch,
+        input_output_aliases={len(operands): 0} if out else {},
+        compiler_params=pltpu.CompilerParams(vmem_limit_bytes=(32 if n > 1 else 24) * 2**20),
         cost_estimate=pl.CostEstimate(
             flops=4 * n * total * KEPT * HALF,
             bytes_accessed=8 * 2**20,
             transcendentals=0,
         ),
-        name="block_rows",
-    )(*operands, *more)
+        name="kept_rows" if keeps else "block_rows",
+    )(*operands, *out, *kept)
 
 
 def next_group(block):
@@ -553,23 +572,27 @@
     second = next_group(first)
     far = [from_chip(first, d) for d in range(1, chips)]
     near_swap = swapped_core(first)
-    far, second = tied(far, second)
     held = [first, near_swap]
     for block in far:
         held += [block, swapped_core(block)]
+    held[0], second = tied(held[0], second)
     far_second = [from_chip(second, d) for d in range(1, chips)]
     near_swap = swapped_core(second)
     live = block_live.reshape(1, OFFS)
 
-    def written(units, held, *more):
-        return correlate(live, turned, tables, rows, chips, units, held, more)
-
-    units = [(0, d) for d in range(chips)] + [(1, 0)]
-    result = written(units, held + [second, near_swap])
+    def written(units, held, **more):
+        return correlate(live, turned, tables, rows, chips, units, held, **more)
+
+    result = written([(0, d) for d in range(chips)], held)
     far_second, result = tied(far_second, result)
+    far_swap = [swapped_core(block) for block in far_second]
+    near = written([(1, 0)], [second, near_swap], keeps=True)
+    far_swap, near = tied(far_swap, near)
+    kept = (near,)
     for d in range(1, chips):
-        far = far_second[d - 1]
-        result = written([(1, d)], [far, swapped_core(far)], result)
+        held = [far_second[d - 1], far_swap[d - 1]]
+        result = written([(1, d)], held, out=(result,), kept=kept)
+        kept = ()
     return result.reshape(-1, OFFS, LAGS)
 
 

time: 38.5 us -> 36.8 us (0.956)
  starting transfers between devices: 6.57 us -> 5.59 us
  Pallas kernels: 17.9 us -> 17.2 us
    ppermute x2, waiting for transfers between devices: 0.01 us -> 4.8 us  [from_chip(): lax.ppermute(block, 'sta', [(i, (i + 2 * distance) % n) for i in range(n)])]
    ppermute x2, waiting for transfers between devices: 11.5 us -> 7.94 us  [next_group(): return lax.ppermute(block, axes, [((i - 1) % n, i) for i in range(n)])]
    ppermute x4, waiting for transfers between devices: 1.34 us -> 0.01 us  [swapped_core(): return lax.ppermute(block, 'sta', [(i, i ^ 1) for i in range(n)])]
    ppermute x2, starting transfers between devices: 2.81 us -> 2.17 us  [from_chip(): lax.ppermute(block, 'sta', [(i, (i + 2 * distance) % n) for i in range(n)])]
    pallas_call x1, Pallas kernels: 5.91 us -> 5.52 us  [spectra(): pl.pallas_call(spectra_kernel, out_shape=jax.ShapeDtypeStruct((2, nw * gr...]
    pallas_call x2 -> x3, Pallas kernels: 9.06 us -> 8.77 us  [correlate(): pl.pallas_call(functools.partial(correlate_kernel, nw, units, (keeps, len...]
  transfers between devices with their start and end apart: 8 -> 8, of which waited for: 3 -> 4; matrix products, arithmetic and copies ran while one was open for 0% -> 0% of each run, Pallas kernels for 25% -> 25%
where the time goes in v4:
time: 36.8 us; the launch traced here: 36.6 us
  Pallas kernels  17.2 us (47%)
  waiting for transfers between devices  12.7 us (35%)
  starting transfers between devices  5.59 us (15%)
  local copies, waits for them, and re-layouts  0.98 us (3%)
    pallas_call x3, Pallas kernels, correlate(): pl.pallas_call(functools.partial(correlate_kernel, nw, units, (keeps, len...  8.77 us
    ppermute x2, waiting for transfers between devices, next_group(): return lax.ppermute(block, axes, [((i - 1) % n, i) for i in range(n)])  7.94 us
    pallas_call x1, Pallas kernels, spectra(): pl.pallas_call(spectra_kernel, out_shape=jax.ShapeDtypeStruct((2, nw * gr...  5.52 us
    ppermute x2, waiting for transfers between devices, from_chip(): lax.ppermute(block, 'sta', [(i, (i + 2 * distance) % n) for i in range(n)])  4.8 us
    ppermute x2, starting transfers between devices, next_group(): return lax.ppermute(block, axes, [((i - 1) % n, i) for i in range(n)])  3.08 us
    ppermute x2, starting transfers between devices, from_chip(): lax.ppermute(block, 'sta', [(i, (i + 2 * distance) % n) for i in range(n)])  2.17 us
    pallas_call x1, Pallas kernels, lag_tables(): pl.pallas_call(lag_kernel, out_shape=[table, table], in_specs=[smem, vmem...  1.63 us
    pallas_call x1, Pallas kernels, prepare(): pl.pallas_call(functools.partial(prepare_kernel, peers), out_shape=jax.Sh...  1.29 us
  transfers between devices with their start and end apart: 8, of which 4 were waited for; matrix products, arithmetic and copies ran while one was open for 0% of the time, Pallas kernels for 25%

profile of v4, /device:TPU:0, one launch (start us, length us, event | category | flops | bytes accessed | tf_op | source)
XLA Modules:
  0.0 36.6 jit_solution(15570807911060759428)
XLA Ops:
  0.0 0.0 copy-start.4
  0.0 5.5 %spectra.1.sent_ref = bf16[2,48,1024]{2,1,0:T(8,128)(2,1)} custom-call(bf16[12,4,16384]{2,1,0:T(4,128)(2,1)} %bitcast.14, f32[1,64]{1,0:T(1,128)} %bitcast.15, s32[2,4]{1,0:T(2,128)} %bitcast.11, s32[1,4]{1,0:T(1,128)} %bitcast.16, bf16[2,512,128]{2,1,0:T(8,128)(2,1)} %constant.12.clone.table_hbm, f32[2,16,256]{2,1,0:T(8,128)} %constant.13.clone.twiddle_hbm, ...), custom_call_target="tpu_custom_call" | custom-call | flops 3000000000 | bytes 5242880 | tf_op jit(solution)/shard_map/spectra/pallas_call | solution.py:289
  5.5 0.0 copy-start
  5.5 3.1 %collective-permute-start = (bf16[2,48,1024]{2,1,0:T(8,128)(2,1)}, bf16[2,48,1024]{2,1,0:T(8,128)(2,1)S(1)}, u32[]{:S(2)}, u32[]{:S(2)}) collective-permute-start(bf16[2,48,1024]{2,1,0:T(8,128)(2,1)} %spectra.1.sent_ref), channel_id=1, source_target_pairs={{28,0},{0,4},{4,8},{8,12},{12,16},{16,20},{20,24},{24,28},{29,1},{... | collective-permute-start | bytes 589832 | tf_op jit(solution)/shard_map/ppermute | solution.py:546
  8.6 0.0 copy-done.4
  8.6 0.0 copy-start.1
  8.6 1.0 %copy-done.1 = bf16[2,48,1024]{2,1,0:T(8,128)(2,1)S(1)} copy-done((bf16[2,48,1024]{2,1,0:T(8,128)(2,1)S(1)}, bf16[2,48,1024]{2,1,0:T(8,128)(2,1)}, u32[]{:S(2)}) %copy-start.1) | copy-done | bytes 196632
  9.6 0.0 copy-start.2
  9.6 0.0 copy-start.3
  9.6 1.3 %prepare.1.turned_ref = bf16[2,4,6,48,1024]{4,3,2,1,0:T(8,128)(2,1)S(1)} custom-call(s32[2,4]{1,0:T(2,128)S(1)} %bitcast.12, bf16[2,48,1024]{2,1,0:T(8,128)(2,1)S(1)} %copy-done.1), custom_call_target="tpu_custom_call" | custom-call | flops 10000000 | bytes 4194304 | tf_op jit(solution)/shard_map/prepare/pallas_call | solution.py:338
  10.9 0.0 copy-done
  10.9 0.0 copy-done.2
  10.9 1.6 %lag_tables.1 = (bf16[1024,512]{1,0:T(8,128)(2,1)S(1)}, bf16[1024,512]{1,0:T(8,128)(2,1)S(1)}) custom-call(s32[2,4]{1,0:T(2,128)S(1)} %bitcast.13, f32[2,256,512]{2,1,0:T(8,128)S(1)} %copy-done, f32[2,16,512]{2,1,0:T(8,128)S(1)} %copy-done.2), custom_call_target="tpu_custom_call" | custom-call | flops 10000000 | bytes 4194304 | tf_op jit(solution)/shard_map/lag_tables/pallas_call | solution.py:372
  12.5 4.2 %collective-permute-done.rest_0_ = bf16[2,48,1024]{2,1,0:T(8,128)(2,1)S(1)} collective-permute-done((bf16[2,48,1024]{2,1,0:T(8,128)(2,1)}, bf16[2,48,1024]{2,1,0:T(8,128)(2,1)S(1)}, u32[]{:S(2)}, u32[]{:S(2)}) %collective-permute-start) | collective-permute-done | bytes 196640 | tf_op jit(solution)/shard_map/ppermute | solution.py:546
  16.7 1.5 %collective-permute-start.4 = (bf16[2,48,1024]{2,1,0:T(8,128)(2,1)S(1)}, bf16[2,48,1024]{2,1,0:T(8,128)(2,1)S(1)}, u32[]{:S(2)}, u32[]{:S(2)}) collective-permute-start(bf16[2,48,1024]{2,1,0:T(8,128)(2,1)S(1)} %collective-permute-done.rest_0_), channel_id=1, source_target_pairs={{0,2},{1,3},{2,0},{3,1},{4,6},{5,7},{6,4},{7,5},{8,10},{9,11},{10,... | collective-permute-start | bytes 589832 | tf_op jit(solution)/shard_map/ppermute | solution.py:556
  18.2 0.0 collective-permute-start.1
  18.2 0.0 collective-permute-start.3
  18.2 4.6 %collective-permute-done.4.rest_2_ = bf16[2,48,1024]{2,1,0:T(8,128)(2,1)S(1)} collective-permute-done((bf16[2,48,1024]{2,1,0:T(8,128)(2,1)S(1)}, bf16[2,48,1024]{2,1,0:T(8,128)(2,1)S(1)}, u32[]{:S(2)}, u32[]{:S(2)}) %collective-permute-start.4) | collective-permute-done | bytes 196640 | tf_op jit(solution)/shard_map/ppermute | solution.py:556
  22.8 0.0 collective-permute-start.5
  22.8 3.8 %collective-permute-done.1.rest_0_ = bf16[2,48,1024]{2,1,0:T(8,128)(2,1)S(1)} collective-permute-done((bf16[2,48,1024]{2,1,0:T(8,128)(2,1)S(1)}, bf16[2,48,1024]{2,1,0:T(8,128)(2,1)S(1)}, u32[]{:S(2)}, u32[]{:S(2)}) %collective-permute-start.1) | collective-permute-done | bytes 196640 | tf_op jit(solution)/shard_map/ppermute | solution.py:546
  26.6 0.7 %collective-permute-start.2 = (bf16[2,48,1024]{2,1,0:T(8,128)(2,1)S(1)}, bf16[2,48,1024]{2,1,0:T(8,128)(2,1)S(1)}, u32[]{:S(2)}, u32[]{:S(2)}) collective-permute-start(bf16[2,48,1024]{2,1,0:T(8,128)(2,1)S(1)} %collective-permute-done.1.rest_0_), channel_id=1, source_target_pairs={{0,2},{1,3},{2,0},{3,1},{4,6},{5,7},{6,4},{7,5},{8,10},{9,11},{10,... | collective-permute-start | bytes 589832 | tf_op jit(solution)/shard_map/ppermute | solution.py:556
  27.2 0.0 collective-permute-start.7
  27.3 0.0 collective-permute-done.3.rest_1_
  27.3 0.0 collective-permute-done.5.rest_3_
  27.3 0.0 copy-done.3
  27.3 4.8 %block_rows.2.rest_2_ = f32[12,2,24,2,1024]{4,3,2,1,0:T(2,128)} custom-call(s32[1,2]{1,0:T(1,128)S(1)} %bitcast.8, bf16[2,4,6,48,1024]{4,3,2,1,0:T(8,128)(2,1)S(1)} %prepare.1.turned_ref, bf16[1024,512]{1,0:T(8,128)(2,1)S(1)} %get-tuple-element.20.even_ref, bf16[1024,512]{1,0:T(8,128)(2,1)S(1)} %get-tuple-element.21.odd_ref, ...), custom_call_target="tpu_custom_call" | custom-call | flops 1207959552 | bytes 8388608 | tf_op jit(solution)/shard_map/block_rows/pallas_call | solution.py:526
  32.0 0.2 collective-permute-done.2.rest_0_
  32.2 0.3 collective-permute-start.6
  32.6 0.0 collective-permute-done.7.rest_1_
  32.6 1.4 %kept_rows.1.rest_3_ = f32[12,24,1024]{2,1,0:T(8,128)S(1)} custom-call(s32[1,2]{1,0:T(1,128)S(1)} %bitcast.9, bf16[2,4,6,48,1024]{4,3,2,1,0:T(8,128)(2,1)S(1)} %prepare.1.turned_ref, bf16[1024,512]{1,0:T(8,128)(2,1)S(1)} %get-tuple-element.20.even_ref, bf16[1024,512]{1,0:T(8,128)(2,1)S(1)} %get-tuple-element.21.odd_ref, ...), custom_call_target="tpu_custom_call" | custom-call | flops 603979776 | bytes 8388608 | tf_op jit(solution)/shard_map/kept_rows/pallas_call | solution.py:526
  33.9 0.0 collective-permute-done.6.rest_1_
  34.0 2.7 %block_rows.3 = f32[12,2,24,2,1024]{4,3,2,1,0:T(2,128)} custom-call(s32[1,2]{1,0:T(1,128)S(1)} %bitcast.10, bf16[2,4,6,48,1024]{4,3,2,1,0:T(8,128)(2,1)S(1)} %prepare.1.turned_ref, bf16[1024,512]{1,0:T(8,128)(2,1)S(1)} %get-tuple-element.20.even_ref, bf16[1024,512]{1,0:T(8,128)(2,1)S(1)} %get-tuple-element.21.odd_ref, ...), custom_call_target="tpu_custom_call", output_to_operand_aliasing={{}: (6, {})} | custom-call | flops 603979776 | bytes 8388608 | tf_op jit(solution)/shard_map/block_rows/pallas_call | solution.py:526
Async XLA Ops:
  0.0 8.6 %copy-start.4 = (s32[4,2]{0,1:T(2,128)S(1)}, s32[4,2]{0,1:T(2,128)}, u32[]{:S(2)}) copy-start(s32[4,2]{0,1:T(2,128)} %param.13) | copy-start | bytes 100
  5.5 5.4 %copy-start = (f32[2,256,512]{2,1,0:T(8,128)S(1)}, f32[2,256,512]{2,1,0:T(8,128)}, u32[]{:S(2)}) copy-start(f32[2,256,512]{2,1,0:T(8,128)} %constant.16.clone.base_ref) | copy-start | bytes 3145732
  5.5 11.2 %collective-permute-start = (bf16[2,48,1024]{2,1,0:T(8,128)(2,1)}, bf16[2,48,1024]{2,1,0:T(8,128)(2,1)S(1)}, u32[]{:S(2)}, u32[]{:S(2)}) collective-permute-start(bf16[2,48,1024]{2,1,0:T(8,128)(2,1)} %spectra.1.sent_ref), channel_id=1, source_target_pairs={{28,0},{0,4},{4,8},{8,12},{12,16},{16,20},{20,24},{24,28},{29,1},{... | collective-permute-start | bytes 589832 | tf_op jit(solution)/shard_map/ppermute | solution.py:546
  8.6 1.0 %copy-start.1 = (bf16[2,48,1024]{2,1,0:T(8,128)(2,1)S(1)}, bf16[2,48,1024]{2,1,0:T(8,128)(2,1)}, u32[]{:S(2)}) copy-start(bf16[2,48,1024]{2,1,0:T(8,128)(2,1)} %spectra.1.sent_ref) | copy-start | bytes 589828
  9.6 1.3 %copy-start.2 = (f32[2,16,512]{2,1,0:T(8,128)S(1)}, f32[2,16,512]{2,1,0:T(8,128)}, u32[]{:S(2)}) copy-start(f32[2,16,512]{2,1,0:T(8,128)} %constant.17.clone.shift_ref) | copy-start | bytes 196612
  9.6 17.7 %copy-start.3 = (s32[2]{0:T(128)S(1)}, s32[2]{0:T(128)}, u32[]{:S(2)}) copy-start(s32[2]{0:T(128)} %param.15) | copy-start | bytes 28
  16.7 6.1 %collective-permute-start.4 = (bf16[2,48,1024]{2,1,0:T(8,128)(2,1)S(1)}, bf16[2,48,1024]{2,1,0:T(8,128)(2,1)S(1)}, u32[]{:S(2)}, u32[]{:S(2)}) collective-permute-start(bf16[2,48,1024]{2,1,0:T(8,128)(2,1)S(1)} %collective-permute-done.rest_0_), channel_id=1, source_target_pairs={{0,2},{1,3},{2,0},{3,1},{4,6},{5,7},{6,4},{7,5},{8,10},{9,11},{10,... | collective-permute-start | bytes 589832 | tf_op jit(solution)/shard_map/ppermute | solution.py:556
  18.2 8.4 %collective-permute-start.1 = (bf16[2,48,1024]{2,1,0:T(8,128)(2,1)S(1)}, bf16[2,48,1024]{2,1,0:T(8,128)(2,1)S(1)}, u32[]{:S(2)}, u32[]{:S(2)}) collective-permute-start(bf16[2,48,1024]{2,1,0:T(8,128)(2,1)S(1)} %collective-permute-done.rest_0_), channel_id=1, source_target_pairs={{28,0},{0,4},{4,8},{8,12},{12,16},{16,20},{20,24},{24,28},{29,1},{... | collective-permute-start | bytes 589832 | tf_op jit(solution)/shard_map/ppermute | solution.py:546
  18.2 9.0 %collective-permute-start.3 = (bf16[2,48,1024]{2,1,0:T(8,128)(2,1)S(1)}, bf16[2,48,1024]{2,1,0:T(8,128)(2,1)S(1)}, u32[]{:S(2)}, u32[]{:S(2)}) collective-permute-start(bf16[2,48,1024]{2,1,0:T(8,128)(2,1)S(1)} %collective-permute-done.rest_0_), channel_id=1, source_target_pairs={{0,1},{1,0},{2,3},{3,2},{4,5},{5,4},{6,7},{7,6},{8,9},{9,8},{10,11... | collective-permute-start | bytes 589832 | tf_op jit(solution)/shard_map/ppermute | solution.py:551
  22.8 4.5 %collective-permute-start.5 = (bf16[2,48,1024]{2,1,0:T(8,128)(2,1)S(1)}, bf16[2,48,1024]{2,1,0:T(8,128)(2,1)S(1)}, u32[]{:S(2)}, u32[]{:S(2)}) collective-permute-start(bf16[2,48,1024]{2,1,0:T(8,128)(2,1)S(1)} %collective-permute-done.4.rest_2_), channel_id=1, source_target_pairs={{0,1},{1,0},{2,3},{3,2},{4,5},{5,4},{6,7},{7,6},{8,9},{9,8},{10,11... | collective-permute-start | bytes 589832 | tf_op jit(solution)/shard_map/ppermute | solution.py:551
  26.6 5.7 %collective-permute-start.2 = (bf16[2,48,1024]{2,1,0:T(8,128)(2,1)S(1)}, bf16[2,48,1024]{2,1,0:T(8,128)(2,1)S(1)}, u32[]{:S(2)}, u32[]{:S(2)}) collective-permute-start(bf16[2,48,1024]{2,1,0:T(8,128)(2,1)S(1)} %collective-permute-done.1.rest_0_), channel_id=1, source_target_pairs={{0,2},{1,3},{2,0},{3,1},{4,6},{5,7},{6,4},{7,5},{8,10},{9,11},{10,... | collective-permute-start | bytes 589832 | tf_op jit(solution)/shard_map/ppermute | solution.py:556
  27.2 5.3 %collective-permute-start.7 = (bf16[2,48,1024]{2,1,0:T(8,128)(2,1)S(1)}, bf16[2,48,1024]{2,1,0:T(8,128)(2,1)S(1)}, u32[]{:S(2)}, u32[]{:S(2)}) collective-permute-start(bf16[2,48,1024]{2,1,0:T(8,128)(2,1)S(1)} %collective-permute-done.1.rest_0_), channel_id=1, source_target_pairs={{0,1},{1,0},{2,3},{3,2},{4,5},{5,4},{6,7},{7,6},{8,9},{9,8},{10,11... | collective-permute-start | bytes 589832 | tf_op jit(solution)/shard_map/ppermute | solution.py:551
  32.2 1.7 %collective-permute-start.6 = (bf16[2,48,1024]{2,1,0:T(8,128)(2,1)S(1)}, bf16[2,48,1024]{2,1,0:T(8,128)(2,1)S(1)}, u32[]{:S(2)}, u32[]{:S(2)}) collective-permute-start(bf16[2,48,1024]{2,1,0:T(8,128)(2,1)S(1)} %collective-permute-done.2.rest_0_), channel_id=1, source_target_pairs={{0,1},{1,0},{2,3},{3,2},{4,5},{5,4},{6,7},{7,6},{8,9},{9,8},{10,11... | collective-permute-start | bytes 589832 | tf_op jit(solution)/shard_map/ppermute | solution.py:551

commit v5 on v4

--- a/solution.py
+++ b/solution.py
@@ -185,13 +185,13 @@
         decimated.append((both[:, :FRAME] + both[:, FRAME:]).astype(bf16).astype(f32))
     each = BLOCKS_IN // PIECES
     copies[1 + PIECES].wait()
-    for at in range(0, ch, 16):
+    for at in range(0, ch, ch):
         d = []
         for b in range(RADIX):
             pair = []
             for frame in (2 * b, 2 * b + 1):
                 row = frame % each * ch + at
-                pair.append(decimated[frame // each][row : row + 16])
+                pair.append(decimated[frame // each][row : row + ch])
             d.append(jnp.concatenate(pair, axis=1))
         y = real_dft16(d)
         for h in range(RADIX):
@@ -204,7 +204,7 @@
                 ur, ui = yr * c - yi * sn, yr * sn + yi * c
             for k, u in enumerate((ur, ui)):
                 where = slice(k * INNER, (k + 1) * INNER)
-                turned[h * ch + at : h * ch + at + 16, where] = u.astype(bf16)
+                turned[h * ch + at : h * ch + at + ch, where] = u.astype(bf16)
 
     for copy in copies[2 + PIECES :]:
         copy.wait()

time: 36.8 us -> 36.8 us (level)
  no operation moved by 1% of the time
where the time goes in v5:
time: 36.8 us; the launch traced here: 36.7 us
  Pallas kernels  17.3 us (47%)
  waiting for transfers between devices  12.8 us (35%)
  starting transfers between devices  5.6 us (15%)
  local copies, waits for them, and re-layouts  0.98 us (3%)
    pallas_call x3, Pallas kernels, correlate(): pl.pallas_call(functools.partial(correlate_kernel, nw, units, (keeps, len...  8.76 us
    ppermute x2, waiting for transfers between devices, next_group(): return lax.ppermute(block, axes, [((i - 1) % n, i) for i in range(n)])  7.93 us
    pallas_call x1, Pallas kernels, spectra(): pl.pallas_call(spectra_kernel, out_shape=jax.ShapeDtypeStruct((2, nw * gr...  5.6 us
    ppermute x2, waiting for transfers between devices, from_chip(): lax.ppermute(block, 'sta', [(i, (i + 2 * distance) % n) for i in range(n)])  4.81 us
    ppermute x2, starting transfers between devices, next_group(): return lax.ppermute(block, axes, [((i - 1) % n, i) for i in range(n)])  3.08 us
    ppermute x2, starting transfers between devices, from_chip(): lax.ppermute(block, 'sta', [(i, (i + 2 * distance) % n) for i in range(n)])  2.17 us
    pallas_call x1, Pallas kernels, lag_tables(): pl.pallas_call(lag_kernel, out_shape=[table, table], in_specs=[smem, vmem...  1.63 us
    pallas_call x1, Pallas kernels, prepare(): pl.pallas_call(functools.partial(prepare_kernel, peers), out_shape=jax.Sh...  1.29 us
  transfers between devices with their start and end apart: 8, of which 4 were waited for; matrix products, arithmetic and copies ran while one was open for 0% of the time, Pallas kernels for 25%

profile of v5, /device:TPU:0, one launch (start us, length us, event | category | flops | bytes accessed | tf_op | source)
XLA Modules:
  0.0 36.7 jit_solution(14212056743219205803)
XLA Ops:
  0.0 0.0 copy-start.4
  0.0 5.6 %spectra.1.sent_ref = bf16[2,48,1024]{2,1,0:T(8,128)(2,1)} custom-call(bf16[12,4,16384]{2,1,0:T(4,128)(2,1)} %bitcast.14, f32[1,64]{1,0:T(1,128)} %bitcast.15, s32[2,4]{1,0:T(2,128)} %bitcast.11, s32[1,4]{1,0:T(1,128)} %bitcast.16, bf16[2,512,128]{2,1,0:T(8,128)(2,1)} %constant.12.clone.table_hbm, f32[2,16,256]{2,1,0:T(8,128)} %constant.13.clone.twiddle_hbm, ...), custom_call_target="tpu_custom_call" | custom-call | flops 3000000000 | bytes 5242880 | tf_op jit(solution)/shard_map/spectra/pallas_call | solution.py:289
  5.6 0.0 copy-start
  5.6 3.1 %collective-permute-start = (bf16[2,48,1024]{2,1,0:T(8,128)(2,1)}, bf16[2,48,1024]{2,1,0:T(8,128)(2,1)S(1)}, u32[]{:S(2)}, u32[]{:S(2)}) collective-permute-start(bf16[2,48,1024]{2,1,0:T(8,128)(2,1)} %spectra.1.sent_ref), channel_id=1, source_target_pairs={{28,0},{0,4},{4,8},{8,12},{12,16},{16,20},{20,24},{24,28},{29,1},{... | collective-permute-start | bytes 589832 | tf_op jit(solution)/shard_map/ppermute | solution.py:546
  8.7 0.0 copy-done.4
  8.7 0.0 copy-start.1
  8.7 1.0 %copy-done.1 = bf16[2,48,1024]{2,1,0:T(8,128)(2,1)S(1)} copy-done((bf16[2,48,1024]{2,1,0:T(8,128)(2,1)S(1)}, bf16[2,48,1024]{2,1,0:T(8,128)(2,1)}, u32[]{:S(2)}) %copy-start.1) | copy-done | bytes 196632
  9.7 0.0 copy-start.2
  9.7 0.0 copy-start.3
  9.7 1.3 %prepare.1.turned_ref = bf16[2,4,6,48,1024]{4,3,2,1,0:T(8,128)(2,1)S(1)} custom-call(s32[2,4]{1,0:T(2,128)S(1)} %bitcast.12, bf16[2,48,1024]{2,1,0:T(8,128)(2,1)S(1)} %copy-done.1), custom_call_target="tpu_custom_call" | custom-call | flops 10000000 | bytes 4194304 | tf_op jit(solution)/shard_map/prepare/pallas_call | solution.py:338
  11.0 0.0 copy-done
  11.0 0.0 copy-done.2
  11.0 1.6 %lag_tables.1 = (bf16[1024,512]{1,0:T(8,128)(2,1)S(1)}, bf16[1024,512]{1,0:T(8,128)(2,1)S(1)}) custom-call(s32[2,4]{1,0:T(2,128)S(1)} %bitcast.13, f32[2,256,512]{2,1,0:T(8,128)S(1)} %copy-done, f32[2,16,512]{2,1,0:T(8,128)S(1)} %copy-done.2), custom_call_target="tpu_custom_call" | custom-call | flops 10000000 | bytes 4194304 | tf_op jit(solution)/shard_map/lag_tables/pallas_call | solution.py:372
  12.6 4.2 %collective-permute-done.rest_0_ = bf16[2,48,1024]{2,1,0:T(8,128)(2,1)S(1)} collective-permute-done((bf16[2,48,1024]{2,1,0:T(8,128)(2,1)}, bf16[2,48,1024]{2,1,0:T(8,128)(2,1)S(1)}, u32[]{:S(2)}, u32[]{:S(2)}) %collective-permute-start) | collective-permute-done | bytes 196640 | tf_op jit(solution)/shard_map/ppermute | solution.py:546
  16.8 1.5 %collective-permute-start.4 = (bf16[2,48,1024]{2,1,0:T(8,128)(2,1)S(1)}, bf16[2,48,1024]{2,1,0:T(8,128)(2,1)S(1)}, u32[]{:S(2)}, u32[]{:S(2)}) collective-permute-start(bf16[2,48,1024]{2,1,0:T(8,128)(2,1)S(1)} %collective-permute-done.rest_0_), channel_id=1, source_target_pairs={{0,2},{1,3},{2,0},{3,1},{4,6},{5,7},{6,4},{7,5},{8,10},{9,11},{10,... | collective-permute-start | bytes 589832 | tf_op jit(solution)/shard_map/ppermute | solution.py:556
  18.3 0.0 collective-permute-start.1
  18.3 0.0 collective-permute-start.3
  18.3 4.6 %collective-permute-done.4.rest_2_ = bf16[2,48,1024]{2,1,0:T(8,128)(2,1)S(1)} collective-permute-done((bf16[2,48,1024]{2,1,0:T(8,128)(2,1)S(1)}, bf16[2,48,1024]{2,1,0:T(8,128)(2,1)S(1)}, u32[]{:S(2)}, u32[]{:S(2)}) %collective-permute-start.4) | collective-permute-done | bytes 196640 | tf_op jit(solution)/shard_map/ppermute | solution.py:556
  22.9 0.0 collective-permute-start.5
  22.9 3.8 %collective-permute-done.1.rest_0_ = bf16[2,48,1024]{2,1,0:T(8,128)(2,1)S(1)} collective-permute-done((bf16[2,48,1024]{2,1,0:T(8,128)(2,1)S(1)}, bf16[2,48,1024]{2,1,0:T(8,128)(2,1)S(1)}, u32[]{:S(2)}, u32[]{:S(2)}) %collective-permute-start.1) | collective-permute-done | bytes 196640 | tf_op jit(solution)/shard_map/ppermute | solution.py:546
  26.6 0.7 %collective-permute-start.2 = (bf16[2,48,1024]{2,1,0:T(8,128)(2,1)S(1)}, bf16[2,48,1024]{2,1,0:T(8,128)(2,1)S(1)}, u32[]{:S(2)}, u32[]{:S(2)}) collective-permute-start(bf16[2,48,1024]{2,1,0:T(8,128)(2,1)S(1)} %collective-permute-done.1.rest_0_), channel_id=1, source_target_pairs={{0,2},{1,3},{2,0},{3,1},{4,6},{5,7},{6,4},{7,5},{8,10},{9,11},{10,... | collective-permute-start | bytes 589832 | tf_op jit(solution)/shard_map/ppermute | solution.py:556
  27.3 0.0 collective-permute-start.7
  27.3 0.0 collective-permute-done.3.rest_1_
  27.3 0.0 collective-permute-done.5.rest_3_
  27.3 0.0 copy-done.3
  27.3 4.7 %block_rows.2.rest_2_ = f32[12,2,24,2,1024]{4,3,2,1,0:T(2,128)} custom-call(s32[1,2]{1,0:T(1,128)S(1)} %bitcast.8, bf16[2,4,6,48,1024]{4,3,2,1,0:T(8,128)(2,1)S(1)} %prepare.1.turned_ref, bf16[1024,512]{1,0:T(8,128)(2,1)S(1)} %get-tuple-element.20.even_ref, bf16[1024,512]{1,0:T(8,128)(2,1)S(1)} %get-tuple-element.21.odd_ref, ...), custom_call_target="tpu_custom_call" | custom-call | flops 1207959552 | bytes 8388608 | tf_op jit(solution)/shard_map/block_rows/pallas_call | solution.py:526
  32.1 0.2 collective-permute-done.2.rest_0_
  32.3 0.3 collective-permute-start.6
  32.7 0.0 collective-permute-done.7.rest_1_
  32.7 1.4 %kept_rows.1.rest_3_ = f32[12,24,1024]{2,1,0:T(8,128)S(1)} custom-call(s32[1,2]{1,0:T(1,128)S(1)} %bitcast.9, bf16[2,4,6,48,1024]{4,3,2,1,0:T(8,128)(2,1)S(1)} %prepare.1.turned_ref, bf16[1024,512]{1,0:T(8,128)(2,1)S(1)} %get-tuple-element.20.even_ref, bf16[1024,512]{1,0:T(8,128)(2,1)S(1)} %get-tuple-element.21.odd_ref, ...), custom_call_target="tpu_custom_call" | custom-call | flops 603979776 | bytes 8388608 | tf_op jit(solution)/shard_map/kept_rows/pallas_call | solution.py:526
  34.0 0.0 collective-permute-done.6.rest_1_
  34.0 2.6 %block_rows.3 = f32[12,2,24,2,1024]{4,3,2,1,0:T(2,128)} custom-call(s32[1,2]{1,0:T(1,128)S(1)} %bitcast.10, bf16[2,4,6,48,1024]{4,3,2,1,0:T(8,128)(2,1)S(1)} %prepare.1.turned_ref, bf16[1024,512]{1,0:T(8,128)(2,1)S(1)} %get-tuple-element.20.even_ref, bf16[1024,512]{1,0:T(8,128)(2,1)S(1)} %get-tuple-element.21.odd_ref, ...), custom_call_target="tpu_custom_call", output_to_operand_aliasing={{}: (6, {})} | custom-call | flops 603979776 | bytes 8388608 | tf_op jit(solution)/shard_map/block_rows/pallas_call | solution.py:526
Async XLA Ops:
  0.0 8.7 %copy-start.4 = (s32[4,2]{0,1:T(2,128)S(1)}, s32[4,2]{0,1:T(2,128)}, u32[]{:S(2)}) copy-start(s32[4,2]{0,1:T(2,128)} %param.13) | copy-start | bytes 100
  5.6 5.4 %copy-start = (f32[2,256,512]{2,1,0:T(8,128)S(1)}, f32[2,256,512]{2,1,0:T(8,128)}, u32[]{:S(2)}) copy-start(f32[2,256,512]{2,1,0:T(8,128)} %constant.16.clone.base_ref) | copy-start | bytes 3145732
  5.6 11.2 %collective-permute-start = (bf16[2,48,1024]{2,1,0:T(8,128)(2,1)}, bf16[2,48,1024]{2,1,0:T(8,128)(2,1)S(1)}, u32[]{:S(2)}, u32[]{:S(2)}) collective-permute-start(bf16[2,48,1024]{2,1,0:T(8,128)(2,1)} %spectra.1.sent_ref), channel_id=1, source_target_pairs={{28,0},{0,4},{4,8},{8,12},{12,16},{16,20},{20,24},{24,28},{29,1},{... | collective-permute-start | bytes 589832 | tf_op jit(solution)/shard_map/ppermute | solution.py:546
  8.7 1.0 %copy-start.1 = (bf16[2,48,1024]{2,1,0:T(8,128)(2,1)S(1)}, bf16[2,48,1024]{2,1,0:T(8,128)(2,1)}, u32[]{:S(2)}) copy-start(bf16[2,48,1024]{2,1,0:T(8,128)(2,1)} %spectra.1.sent_ref) | copy-start | bytes 589828
  9.7 1.3 %copy-start.2 = (f32[2,16,512]{2,1,0:T(8,128)S(1)}, f32[2,16,512]{2,1,0:T(8,128)}, u32[]{:S(2)}) copy-start(f32[2,16,512]{2,1,0:T(8,128)} %constant.17.clone.shift_ref) | copy-start | bytes 196612
  9.7 17.7 %copy-start.3 = (s32[2]{0:T(128)S(1)}, s32[2]{0:T(128)}, u32[]{:S(2)}) copy-start(s32[2]{0:T(128)} %param.15) | copy-start | bytes 28
  16.8 6.1 %collective-permute-start.4 = (bf16[2,48,1024]{2,1,0:T(8,128)(2,1)S(1)}, bf16[2,48,1024]{2,1,0:T(8,128)(2,1)S(1)}, u32[]{:S(2)}, u32[]{:S(2)}) collective-permute-start(bf16[2,48,1024]{2,1,0:T(8,128)(2,1)S(1)} %collective-permute-done.rest_0_), channel_id=1, source_target_pairs={{0,2},{1,3},{2,0},{3,1},{4,6},{5,7},{6,4},{7,5},{8,10},{9,11},{10,... | collective-permute-start | bytes 589832 | tf_op jit(solution)/shard_map/ppermute | solution.py:556
  18.3 8.4 %collective-permute-start.1 = (bf16[2,48,1024]{2,1,0:T(8,128)(2,1)S(1)}, bf16[2,48,1024]{2,1,0:T(8,128)(2,1)S(1)}, u32[]{:S(2)}, u32[]{:S(2)}) collective-permute-start(bf16[2,48,1024]{2,1,0:T(8,128)(2,1)S(1)} %collective-permute-done.rest_0_), channel_id=1, source_target_pairs={{28,0},{0,4},{4,8},{8,12},{12,16},{16,20},{20,24},{24,28},{29,1},{... | collective-permute-start | bytes 589832 | tf_op jit(solution)/shard_map/ppermute | solution.py:546
  18.3 9.0 %collective-permute-start.3 = (bf16[2,48,1024]{2,1,0:T(8,128)(2,1)S(1)}, bf16[2,48,1024]{2,1,0:T(8,128)(2,1)S(1)}, u32[]{:S(2)}, u32[]{:S(2)}) collective-permute-start(bf16[2,48,1024]{2,1,0:T(8,128)(2,1)S(1)} %collective-permute-done.rest_0_), channel_id=1, source_target_pairs={{0,1},{1,0},{2,3},{3,2},{4,5},{5,4},{6,7},{7,6},{8,9},{9,8},{10,11... | collective-permute-start | bytes 589832 | tf_op jit(solution)/shard_map/ppermute | solution.py:551
  22.9 4.5 %collective-permute-start.5 = (bf16[2,48,1024]{2,1,0:T(8,128)(2,1)S(1)}, bf16[2,48,1024]{2,1,0:T(8,128)(2,1)S(1)}, u32[]{:S(2)}, u32[]{:S(2)}) collective-permute-start(bf16[2,48,1024]{2,1,0:T(8,128)(2,1)S(1)} %collective-permute-done.4.rest_2_), channel_id=1, source_target_pairs={{0,1},{1,0},{2,3},{3,2},{4,5},{5,4},{6,7},{7,6},{8,9},{9,8},{10,11... | collective-permute-start | bytes 589832 | tf_op jit(solution)/shard_map/ppermute | solution.py:551
  26.6 5.7 %collective-permute-start.2 = (bf16[2,48,1024]{2,1,0:T(8,128)(2,1)S(1)}, bf16[2,48,1024]{2,1,0:T(8,128)(2,1)S(1)}, u32[]{:S(2)}, u32[]{:S(2)}) collective-permute-start(bf16[2,48,1024]{2,1,0:T(8,128)(2,1)S(1)} %collective-permute-done.1.rest_0_), channel_id=1, source_target_pairs={{0,2},{1,3},{2,0},{3,1},{4,6},{5,7},{6,4},{7,5},{8,10},{9,11},{10,... | collective-permute-start | bytes 589832 | tf_op jit(solution)/shard_map/ppermute | solution.py:556
  27.3 5.3 %collective-permute-start.7 = (bf16[2,48,1024]{2,1,0:T(8,128)(2,1)S(1)}, bf16[2,48,1024]{2,1,0:T(8,128)(2,1)S(1)}, u32[]{:S(2)}, u32[]{:S(2)}) collective-permute-start(bf16[2,48,1024]{2,1,0:T(8,128)(2,1)S(1)} %collective-permute-done.1.rest_0_), channel_id=1, source_target_pairs={{0,1},{1,0},{2,3},{3,2},{4,5},{5,4},{6,7},{7,6},{8,9},{9,8},{10,11... | collective-permute-start | bytes 589832 | tf_op jit(solution)/shard_map/ppermute | solution.py:551
  32.3 1.7 %collective-permute-start.6 = (bf16[2,48,1024]{2,1,0:T(8,128)(2,1)S(1)}, bf16[2,48,1024]{2,1,0:T(8,128)(2,1)S(1)}, u32[]{:S(2)}, u32[]{:S(2)}) collective-permute-start(bf16[2,48,1024]{2,1,0:T(8,128)(2,1)S(1)} %collective-permute-done.2.rest_0_), channel_id=1, source_target_pairs={{0,1},{1,0},{2,3},{3,2},{4,5},{5,4},{6,7},{7,6},{8,9},{9,8},{10,11... | collective-permute-start | bytes 589832 | tf_op jit(solution)/shard_map/ppermute | solution.py:551

commit v6 on v4

--- a/solution.py
+++ b/solution.py
@@ -500,7 +500,10 @@
             if at < len(units):
                 for band in range(NBANDS):
                     cross(at, band)
-            if at:
+            if at == len(units):
+                for step in range(2):
+                    finished(at - 1, step * width, width)
+            elif at:
                 finished(at - 1, 0, HALF)
     for copy in copies:
         copy.wait()

time: 36.8 us -> 37 us (level)
  transfers between devices with their start and end apart: 8 -> 8, of which waited for: 4 -> 3; matrix products, arithmetic and copies ran while one was open for 0% -> 0% of each run, Pallas kernels for 25% -> 25%
where the time goes in v6:
time: 37 us; the launch traced here: 36.9 us
  Pallas kernels  17.5 us (47%)
  waiting for transfers between devices  12.5 us (34%)
  starting transfers between devices  5.81 us (16%)
  local copies, waits for them, and re-layouts  0.98 us (3%)
    pallas_call x3, Pallas kernels, correlate(): pl.pallas_call(functools.partial(correlate_kernel, nw, units, (keeps, len...  9.02 us
    ppermute x2, waiting for transfers between devices, next_group(): return lax.ppermute(block, axes, [((i - 1) % n, i) for i in range(n)])  7.94 us
    pallas_call x1, Pallas kernels, spectra(): pl.pallas_call(spectra_kernel, out_shape=jax.ShapeDtypeStruct((2, nw * gr...  5.52 us
    ppermute x2, waiting for transfers between devices, from_chip(): lax.ppermute(block, 'sta', [(i, (i + 2 * distance) % n) for i in range(n)])  4.6 us
    ppermute x2, starting transfers between devices, next_group(): return lax.ppermute(block, axes, [((i - 1) % n, i) for i in range(n)])  3.08 us
    ppermute x2, starting transfers between devices, from_chip(): lax.ppermute(block, 'sta', [(i, (i + 2 * distance) % n) for i in range(n)])  2.17 us
    pallas_call x1, Pallas kernels, lag_tables(): pl.pallas_call(lag_kernel, out_shape=[table, table], in_specs=[smem, vmem...  1.63 us
    pallas_call x1, Pallas kernels, prepare(): pl.pallas_call(functools.partial(prepare_kernel, peers), out_shape=jax.Sh...  1.29 us
  transfers between devices with their start and end apart: 8, of which 3 were waited for; matrix products, arithmetic and copies ran while one was open for 0% of the time, Pallas kernels for 25%

profile of v6, /device:TPU:0, one launch (start us, length us, event | category | flops | bytes accessed | tf_op | source)
XLA Modules:
  0.0 36.9 jit_solution(15037796969833013817)
XLA Ops:
  0.0 0.0 copy-start.4
  0.0 5.5 %spectra.1.sent_ref = bf16[2,48,1024]{2,1,0:T(8,128)(2,1)} custom-call(bf16[12,4,16384]{2,1,0:T(4,128)(2,1)} %bitcast.14, f32[1,64]{1,0:T(1,128)} %bitcast.15, s32[2,4]{1,0:T(2,128)} %bitcast.11, s32[1,4]{1,0:T(1,128)} %bitcast.16, bf16[2,512,128]{2,1,0:T(8,128)(2,1)} %constant.12.clone.table_hbm, f32[2,16,256]{2,1,0:T(8,128)} %constant.13.clone.twiddle_hbm, ...), custom_call_target="tpu_custom_call" | custom-call | flops 3000000000 | bytes 5242880 | tf_op jit(solution)/shard_map/spectra/pallas_call | solution.py:289
  5.5 0.0 copy-start
  5.5 3.1 %collective-permute-start = (bf16[2,48,1024]{2,1,0:T(8,128)(2,1)}, bf16[2,48,1024]{2,1,0:T(8,128)(2,1)S(1)}, u32[]{:S(2)}, u32[]{:S(2)}) collective-permute-start(bf16[2,48,1024]{2,1,0:T(8,128)(2,1)} %spectra.1.sent_ref), channel_id=1, source_target_pairs={{28,0},{0,4},{4,8},{8,12},{12,16},{16,20},{20,24},{24,28},{29,1},{... | collective-permute-start | bytes 589832 | tf_op jit(solution)/shard_map/ppermute | solution.py:549
  8.6 0.0 copy-done.4
  8.6 0.0 copy-start.1
  8.6 1.0 %copy-done.1 = bf16[2,48,1024]{2,1,0:T(8,128)(2,1)S(1)} copy-done((bf16[2,48,1024]{2,1,0:T(8,128)(2,1)S(1)}, bf16[2,48,1024]{2,1,0:T(8,128)(2,1)}, u32[]{:S(2)}) %copy-start.1) | copy-done | bytes 196632
  9.6 0.0 copy-start.2
  9.6 0.0 copy-start.3
  9.6 1.3 %prepare.1.turned_ref = bf16[2,4,6,48,1024]{4,3,2,1,0:T(8,128)(2,1)S(1)} custom-call(s32[2,4]{1,0:T(2,128)S(1)} %bitcast.12, bf16[2,48,1024]{2,1,0:T(8,128)(2,1)S(1)} %copy-done.1), custom_call_target="tpu_custom_call" | custom-call | flops 10000000 | bytes 4194304 | tf_op jit(solution)/shard_map/prepare/pallas_call | solution.py:338
  10.9 0.0 copy-done
  10.9 0.0 copy-done.2
  10.9 1.6 %lag_tables.1 = (bf16[1024,512]{1,0:T(8,128)(2,1)S(1)}, bf16[1024,512]{1,0:T(8,128)(2,1)S(1)}) custom-call(s32[2,4]{1,0:T(2,128)S(1)} %bitcast.13, f32[2,256,512]{2,1,0:T(8,128)S(1)} %copy-done, f32[2,16,512]{2,1,0:T(8,128)S(1)} %copy-done.2), custom_call_target="tpu_custom_call" | custom-call | flops 10000000 | bytes 4194304 | tf_op jit(solution)/shard_map/lag_tables/pallas_call | solution.py:372
  12.5 4.2 %collective-permute-done.rest_0_ = bf16[2,48,1024]{2,1,0:T(8,128)(2,1)S(1)} collective-permute-done((bf16[2,48,1024]{2,1,0:T(8,128)(2,1)}, bf16[2,48,1024]{2,1,0:T(8,128)(2,1)S(1)}, u32[]{:S(2)}, u32[]{:S(2)}) %collective-permute-start) | collective-permute-done | bytes 196640 | tf_op jit(solution)/shard_map/ppermute | solution.py:549
  16.7 1.5 %collective-permute-start.4 = (bf16[2,48,1024]{2,1,0:T(8,128)(2,1)S(1)}, bf16[2,48,1024]{2,1,0:T(8,128)(2,1)S(1)}, u32[]{:S(2)}, u32[]{:S(2)}) collective-permute-start(bf16[2,48,1024]{2,1,0:T(8,128)(2,1)S(1)} %collective-permute-done.rest_0_), channel_id=1, source_target_pairs={{0,2},{1,3},{2,0},{3,1},{4,6},{5,7},{6,4},{7,5},{8,10},{9,11},{10,... | collective-permute-start | bytes 589832 | tf_op jit(solution)/shard_map/ppermute | solution.py:559
  18.2 0.0 collective-permute-start.1
  18.2 0.0 collective-permute-start.3
  18.2 4.6 %collective-permute-done.4.rest_2_ = bf16[2,48,1024]{2,1,0:T(8,128)(2,1)S(1)} collective-permute-done((bf16[2,48,1024]{2,1,0:T(8,128)(2,1)S(1)}, bf16[2,48,1024]{2,1,0:T(8,128)(2,1)S(1)}, u32[]{:S(2)}, u32[]{:S(2)}) %collective-permute-start.4) | collective-permute-done | bytes 196640 | tf_op jit(solution)/shard_map/ppermute | solution.py:559
  22.8 0.0 collective-permute-start.5
  22.8 3.8 %collective-permute-done.1.rest_0_ = bf16[2,48,1024]{2,1,0:T(8,128)(2,1)S(1)} collective-permute-done((bf16[2,48,1024]{2,1,0:T(8,128)(2,1)S(1)}, bf16[2,48,1024]{2,1,0:T(8,128)(2,1)S(1)}, u32[]{:S(2)}, u32[]{:S(2)}) %collective-permute-start.1) | collective-permute-done | bytes 196640 | tf_op jit(solution)/shard_map/ppermute | solution.py:549
  26.6 0.7 %collective-permute-start.2 = (bf16[2,48,1024]{2,1,0:T(8,128)(2,1)S(1)}, bf16[2,48,1024]{2,1,0:T(8,128)(2,1)S(1)}, u32[]{:S(2)}, u32[]{:S(2)}) collective-permute-start(bf16[2,48,1024]{2,1,0:T(8,128)(2,1)S(1)} %collective-permute-done.1.rest_0_), channel_id=1, source_target_pairs={{0,2},{1,3},{2,0},{3,1},{4,6},{5,7},{6,4},{7,5},{8,10},{9,11},{10,... | collective-permute-start | bytes 589832 | tf_op jit(solution)/shard_map/ppermute | solution.py:559
  27.2 0.0 collective-permute-start.7
  27.3 0.0 collective-permute-done.3.rest_1_
  27.3 0.0 collective-permute-done.5.rest_3_
  27.3 0.0 copy-done.3
  27.3 5.0 %block_rows.2.rest_2_ = f32[12,2,24,2,1024]{4,3,2,1,0:T(2,128)} custom-call(s32[1,2]{1,0:T(1,128)S(1)} %bitcast.8, bf16[2,4,6,48,1024]{4,3,2,1,0:T(8,128)(2,1)S(1)} %prepare.1.turned_ref, bf16[1024,512]{1,0:T(8,128)(2,1)S(1)} %get-tuple-element.20.even_ref, bf16[1024,512]{1,0:T(8,128)(2,1)S(1)} %get-tuple-element.21.odd_ref, ...), custom_call_target="tpu_custom_call" | custom-call | flops 1207959552 | bytes 8388608 | tf_op jit(solution)/shard_map/block_rows/pallas_call | solution.py:529
  32.3 0.0 collective-permute-done.2.rest_0_
  32.3 0.6 %collective-permute-start.6 = (bf16[2,48,1024]{2,1,0:T(8,128)(2,1)S(1)}, bf16[2,48,1024]{2,1,0:T(8,128)(2,1)S(1)}, u32[]{:S(2)}, u32[]{:S(2)}) collective-permute-start(bf16[2,48,1024]{2,1,0:T(8,128)(2,1)S(1)} %collective-permute-done.2.rest_0_), channel_id=1, source_target_pairs={{0,1},{1,0},{2,3},{3,2},{4,5},{5,4},{6,7},{7,6},{8,9},{9,8},{10,11... | collective-permute-start | bytes 589832 | tf_op jit(solution)/shard_map/ppermute | solution.py:554
  32.8 0.0 collective-permute-done.7.rest_1_
  32.9 1.4 %kept_rows.1.rest_3_ = f32[12,24,1024]{2,1,0:T(8,128)S(1)} custom-call(s32[1,2]{1,0:T(1,128)S(1)} %bitcast.9, bf16[2,4,6,48,1024]{4,3,2,1,0:T(8,128)(2,1)S(1)} %prepare.1.turned_ref, bf16[1024,512]{1,0:T(8,128)(2,1)S(1)} %get-tuple-element.20.even_ref, bf16[1024,512]{1,0:T(8,128)(2,1)S(1)} %get-tuple-element.21.odd_ref, ...), custom_call_target="tpu_custom_call" | custom-call | flops 603979776 | bytes 8388608 | tf_op jit(solution)/shard_map/kept_rows/pallas_call | solution.py:529
  34.2 0.0 collective-permute-done.6.rest_1_
  34.2 2.7 %block_rows.3 = f32[12,2,24,2,1024]{4,3,2,1,0:T(2,128)} custom-call(s32[1,2]{1,0:T(1,128)S(1)} %bitcast.10, bf16[2,4,6,48,1024]{4,3,2,1,0:T(8,128)(2,1)S(1)} %prepare.1.turned_ref, bf16[1024,512]{1,0:T(8,128)(2,1)S(1)} %get-tuple-element.20.even_ref, bf16[1024,512]{1,0:T(8,128)(2,1)S(1)} %get-tuple-element.21.odd_ref, ...), custom_call_target="tpu_custom_call", output_to_operand_aliasing={{}: (6, {})} | custom-call | flops 603979776 | bytes 8388608 | tf_op jit(solution)/shard_map/block_rows/pallas_call | solution.py:529
Async XLA Ops:
  0.0 8.6 %copy-start.4 = (s32[4,2]{0,1:T(2,128)S(1)}, s32[4,2]{0,1:T(2,128)}, u32[]{:S(2)}) copy-start(s32[4,2]{0,1:T(2,128)} %param.13) | copy-start | bytes 100
  5.5 5.4 %copy-start = (f32[2,256,512]{2,1,0:T(8,128)S(1)}, f32[2,256,512]{2,1,0:T(8,128)}, u32[]{:S(2)}) copy-start(f32[2,256,512]{2,1,0:T(8,128)} %constant.16.clone.base_ref) | copy-start | bytes 3145732
  5.5 11.2 %collective-permute-start = (bf16[2,48,1024]{2,1,0:T(8,128)(2,1)}, bf16[2,48,1024]{2,1,0:T(8,128)(2,1)S(1)}, u32[]{:S(2)}, u32[]{:S(2)}) collective-permute-start(bf16[2,48,1024]{2,1,0:T(8,128)(2,1)} %spectra.1.sent_ref), channel_id=1, source_target_pairs={{28,0},{0,4},{4,8},{8,12},{12,16},{16,20},{20,24},{24,28},{29,1},{... | collective-permute-start | bytes 589832 | tf_op jit(solution)/shard_map/ppermute | solution.py:549
  8.6 1.0 %copy-start.1 = (bf16[2,48,1024]{2,1,0:T(8,128)(2,1)S(1)}, bf16[2,48,1024]{2,1,0:T(8,128)(2,1)}, u32[]{:S(2)}) copy-start(bf16[2,48,1024]{2,1,0:T(8,128)(2,1)} %spectra.1.sent_ref) | copy-start | bytes 589828
  9.6 1.3 %copy-start.2 = (f32[2,16,512]{2,1,0:T(8,128)S(1)}, f32[2,16,512]{2,1,0:T(8,128)}, u32[]{:S(2)}) copy-start(f32[2,16,512]{2,1,0:T(8,128)} %constant.17.clone.shift_ref) | copy-start | bytes 196612
  9.6 17.7 %copy-start.3 = (s32[2]{0:T(128)S(1)}, s32[2]{0:T(128)}, u32[]{:S(2)}) copy-start(s32[2]{0:T(128)} %param.15) | copy-start | bytes 28
  16.7 6.1 %collective-permute-start.4 = (bf16[2,48,1024]{2,1,0:T(8,128)(2,1)S(1)}, bf16[2,48,1024]{2,1,0:T(8,128)(2,1)S(1)}, u32[]{:S(2)}, u32[]{:S(2)}) collective-permute-start(bf16[2,48,1024]{2,1,0:T(8,128)(2,1)S(1)} %collective-permute-done.rest_0_), channel_id=1, source_target_pairs={{0,2},{1,3},{2,0},{3,1},{4,6},{5,7},{6,4},{7,5},{8,10},{9,11},{10,... | collective-permute-start | bytes 589832 | tf_op jit(solution)/shard_map/ppermute | solution.py:559
  18.2 8.4 %collective-permute-start.1 = (bf16[2,48,1024]{2,1,0:T(8,128)(2,1)S(1)}, bf16[2,48,1024]{2,1,0:T(8,128)(2,1)S(1)}, u32[]{:S(2)}, u32[]{:S(2)}) collective-permute-start(bf16[2,48,1024]{2,1,0:T(8,128)(2,1)S(1)} %collective-permute-done.rest_0_), channel_id=1, source_target_pairs={{28,0},{0,4},{4,8},{8,12},{12,16},{16,20},{20,24},{24,28},{29,1},{... | collective-permute-start | bytes 589832 | tf_op jit(solution)/shard_map/ppermute | solution.py:549
  18.2 9.0 %collective-permute-start.3 = (bf16[2,48,1024]{2,1,0:T(8,128)(2,1)S(1)}, bf16[2,48,1024]{2,1,0:T(8,128)(2,1)S(1)}, u32[]{:S(2)}, u32[]{:S(2)}) collective-permute-start(bf16[2,48,1024]{2,1,0:T(8,128)(2,1)S(1)} %collective-permute-done.rest_0_), channel_id=1, source_target_pairs={{0,1},{1,0},{2,3},{3,2},{4,5},{5,4},{6,7},{7,6},{8,9},{9,8},{10,11... | collective-permute-start | bytes 589832 | tf_op jit(solution)/shard_map/ppermute | solution.py:554
  22.8 4.5 %collective-permute-start.5 = (bf16[2,48,1024]{2,1,0:T(8,128)(2,1)S(1)}, bf16[2,48,1024]{2,1,0:T(8,128)(2,1)S(1)}, u32[]{:S(2)}, u32[]{:S(2)}) collective-permute-start(bf16[2,48,1024]{2,1,0:T(8,128)(2,1)S(1)} %collective-permute-done.4.rest_2_), channel_id=1, source_target_pairs={{0,1},{1,0},{2,3},{3,2},{4,5},{5,4},{6,7},{7,6},{8,9},{9,8},{10,11... | collective-permute-start | bytes 589832 | tf_op jit(solution)/shard_map/ppermute | solution.py:554
  26.6 5.7 %collective-permute-start.2 = (bf16[2,48,1024]{2,1,0:T(8,128)(2,1)S(1)}, bf16[2,48,1024]{2,1,0:T(8,128)(2,1)S(1)}, u32[]{:S(2)}, u32[]{:S(2)}) collective-permute-start(bf16[2,48,1024]{2,1,0:T(8,128)(2,1)S(1)} %collective-permute-done.1.rest_0_), channel_id=1, source_target_pairs={{0,2},{1,3},{2,0},{3,1},{4,6},{5,7},{6,4},{7,5},{8,10},{9,11},{10,... | collective-permute-start | bytes 589832 | tf_op jit(solution)/shard_map/ppermute | solution.py:559
  27.2 5.6 %collective-permute-start.7 = (bf16[2,48,1024]{2,1,0:T(8,128)(2,1)S(1)}, bf16[2,48,1024]{2,1,0:T(8,128)(2,1)S(1)}, u32[]{:S(2)}, u32[]{:S(2)}) collective-permute-start(bf16[2,48,1024]{2,1,0:T(8,128)(2,1)S(1)} %collective-permute-done.1.rest_0_), channel_id=1, source_target_pairs={{0,1},{1,0},{2,3},{3,2},{4,5},{5,4},{6,7},{7,6},{8,9},{9,8},{10,11... | collective-permute-start | bytes 589832 | tf_op jit(solution)/shard_map/ppermute | solution.py:554
  32.3 1.9 %collective-permute-start.6 = (bf16[2,48,1024]{2,1,0:T(8,128)(2,1)S(1)}, bf16[2,48,1024]{2,1,0:T(8,128)(2,1)S(1)}, u32[]{:S(2)}, u32[]{:S(2)}) collective-permute-start(bf16[2,48,1024]{2,1,0:T(8,128)(2,1)S(1)} %collective-permute-done.2.rest_0_), channel_id=1, source_target_pairs={{0,1},{1,0},{2,3},{3,2},{4,5},{5,4},{6,7},{7,6},{8,9},{9,8},{10,11... | collective-permute-start | bytes 589832 | tf_op jit(solution)/shard_map/ppermute | solution.py:554
